TPU v7x, 32 devices: a whole 2x2x4 slice. The times are simulated.
32 devices in a mesh: groups: 2 (over y), bx: 4 (over z), by: 2 (over x), bz: 2 (over core).
Axes of the slice: x: 2, y: 2, z: 4, core: 2. Of those that a mesh axis runs over, the one named last changes fastest.
Arguments:
- slab: float32 [4, 512, 1024], P(('groups', 'bz'), 'bx', 'by'), parts along dimension 0, may hold values from -6 to 6
- plane_test: float32 [2, 256], P('bz'), may hold values from -4 to 4
- row_test: float32 [512, 256], P('bx'), may hold values from -0.25 to 0.25
- col_test: float32 [1024, 256], P('by'), may hold values from -0.1875 to 0.1875
- core_planes: float32 [512, 2], P('bz'), may hold values from -4 to 4
- core_rows: float32 [512, 512], P(None, 'bx'), may hold values from -0.25 to 0.25
- core_cols: float32 [512, 1024], P(None, 'by'), may hold values from -0.1875 to 0.1875
Outputs:
- plane_sketch: float32 [4, 256], P(('groups', 'bz')), parts along dimension 0
- row_sketch: float32 [1024, 256], P(('groups', 'bx'), ('by', 'bz')), parts along dimension 0
- col_sketch: float32 [2048, 256], P(('groups', 'by'), ('bx', 'bz')), parts along dimension 0
- core_sketch: float32 [1024, 512, 512], P(('groups', 'bz'), 'bx', 'by'), parts along dimension 0
There are 2 independent parts, one for each index of `groups`. A program takes and returns all parts, laid end to end along the dimension named above; an argument that names none is the same for every part. Nothing has to cross between parts.
All inputs are finite; a program needn't handle non-finite values.
Results may differ from a plain program's by a relative error of at most 0.00011.
Values sent between devices are 32-bit elements; how exact they have to be, the bound alone decides.
No kernel may reach another device: no remote copies, remote signals or barrier semaphores. Data moves between devices by JAX's collectives and lax.ppermute only.
A program may use at most 128 MiB of HBM per device.

v0:
```python
import jax
import jax.numpy as jnp
from jax import lax
from jax.sharding import PartitionSpec as P


def on_device(slab, plane_test, row_test, col_test, core_planes, core_rows, core_cols):
    highest = lax.Precision.HIGHEST
    by_col = jnp.einsum("pij,jr->pir", slab, col_test, precision=highest)
    plane_part = jnp.einsum("pir,ir->pr", by_col, row_test, precision=highest)
    row_part = jnp.einsum("pir,pr->ir", by_col, plane_test, precision=highest)
    by_row = jnp.einsum("pij,ir->pjr", slab, row_test, precision=highest)
    col_part = jnp.einsum("pjr,pr->jr", by_row, plane_test, precision=highest)
    plane_sketch = lax.psum(plane_part, ("bx", "by"))
    row_sketch = lax.psum_scatter(row_part, ("by", "bz"), scatter_dimension=1, tiled=True)
    col_sketch = lax.psum_scatter(col_part, ("bx", "bz"), scatter_dimension=1, tiled=True)
    shrunk = jnp.einsum("pij,bj->pib", slab, core_cols, precision=highest)
    reduced = lax.psum_scatter(shrunk, "by", scatter_dimension=2, tiled=True)
    partial_value = jnp.einsum("pib,ai->pab", reduced, core_rows, precision=highest)
    partial_value = lax.psum_scatter(partial_value, "bx", scatter_dimension=1, tiled=True)
    core_sketch = jnp.einsum(
        "cp,pab->cab",
        core_planes,
        lax.all_gather(partial_value, "bz", axis=0, tiled=True),
        precision=highest,
    )
    return (plane_sketch, row_sketch, col_sketch, core_sketch)


def solution(mesh):
    in_specs = (
        P(("groups", "bz"), "bx", "by"),
        P("bz", None),
        P("bx", None),
        P("by", None),
        P("bz", None),
        P(None, "bx"),
        P(None, "by"),
    )
    out_specs = (
        P(("groups", "bz"), None),
        P(("groups", "bx"), ("by", "bz")),
        P(("groups", "by"), ("bx", "bz")),
        P(("groups", "bz"), "bx", "by"),
    )
    return jax.shard_map(
        on_device, mesh=mesh, in_specs=in_specs, out_specs=out_specs, check_vma=False
    )
```

profile of v0, /device:TPU:0, one launch (start us, length us, event | category | flops | bytes accessed | tf_op | source)
XLA Modules:
  0.0 129.5 jit_solution(7191022147818254434)
XLA Ops:
  7.2 0.0 copy-start
  7.2 0.0 reduce-scatter.9.cloned.1.call-start
  7.2 1.2 copy-done
  8.4 2.8 %convolution_bitcast_fusion.2 = f32[1,128,512]{2,1,0:T(8,128)} fusion(f32[512,512]{1,0:T(8,128)S(1)} %copy-done, f32[1,128,512]{2,1,0:T(8,128)} %param.7), kind=kOutput, calls=%fused_computation.4 | convolution fusion | flops 402653184 | bytes 1572864 | tf_op jit(solution)/shard_map/pij,bj->pib/dot_general | solution.py:17
  11.2 0.0 reduce-scatter.9.cloned.1.call-update
  11.2 0.0 reduce-scatter.11.cloned.1.call-start
  11.3 14.5 %reduce-scatter.9.cloned.1.call-done = f32[1,128,256]{2,1,0:T(8,128)} async-done(((f32[1,128,512]{2,1,0:T(8,128)}), f32[1,128,256]{2,1,0:T(8,128)}) %reduce-scatter.9.cloned.1.call-update) | async-done | bytes 131088 | tf_op jit(solution)/shard_map/reduce_scatter | solution.py:18
  25.8 2.4 %convolution_bitcast_fusion.1 = f32[1,512,256]{1,2,0:T(8,128)} fusion(f32[512,128]{1,0:T(8,128)} %param.12, f32[1,128,256]{2,1,0:T(8,128)} %reduce-scatter.9.cloned.1.call-done), kind=kOutput, calls=%fused_computation.1 | convolution fusion | flops 201326592 | bytes 917504 | tf_op jit(solution)/shard_map/pib,ai->pab/dot_general | solution.py:19
  28.2 0.0 reduce-scatter.11.cloned.1.call-update
  28.2 0.0 reduce-scatter.13.cloned.1.call-start
  28.3 1.6 %multiply_reduce_fusion = (f32[256]{0:T(256)S(1)}, f32[128,256]{1,0:T(8,128)S(1)}) fusion(f32[128,256]{1,0:T(8,128)} %param.9, f32[512,256]{1,0:T(8,128)} %param.10, f32[1,128,512]{2,1,0:T(8,128)} %param.7), kind=kOutput, calls=%fused_computation.11 | convolution fusion | flops 201391872 | bytes 1049600 | tf_op jit(solution)/shard_map/pij,jr->pir/dot_general | solution.py:9
  29.9 0.7 broadcast_multiply_fusion
  30.5 0.7 copy.24
  31.3 0.0 reduce-scatter.13.cloned.1.call-update
  31.3 0.0 reduce-scatter.7.cloned.1.call-start
  31.4 2.4 %fusion = f32[512,256]{0,1:T(8,128)} fusion(f32[128,256]{1,0:T(8,128)} %param.9, f32[1,128,512]{2,1,0:T(8,128)} %param.7, f32[256]{0:T(256)} %bitcast.40), kind=kOutput, calls=%fused_computation.3 | convolution fusion | flops 201457664 | bytes 918528 | tf_op jit(solution)/shard_map/pij,ir->pjr/dot_general | solution.py:12
  33.8 0.0 reduce-scatter.7.cloned.1.call-update
  33.8 21.1 %psum.7 = f32[1,256]{1,0:T(1,128)} all-reduce(f32[1,256]{1,0:T(1,128)S(1)} %bitcast.38), channel_id=1, replica_groups=mesh['groups'=2,'bx'=4,'by'=2,'bz'=2] {'bx','by'}, use_global_device_ids=true, to_apply=%region_0.0 | all-reduce | flops 256 | bytes 2048 | tf_op jit(solution)/shard_map/psum | solution.py:14
  54.9 0.0 reduce-scatter.11.cloned.1.call-done
  54.9 1.0 copy.14
  55.9 2.0 %all_gather.3 = f32[2,128,256]{2,1,0:T(8,128)S(1)} all-gather(f32[1,128,256]{2,1,0:T(8,128)S(1)} %copy.14), channel_id=1, replica_groups=mesh['groups'=2,'bx'=4,'by'=2,'bz'=2] {'bz'}, dimensions={0}, use_global_device_ids=true | all-gather | bytes 393216 | tf_op jit(solution)/shard_map/all_gather | solution.py:24
  57.9 0.0 copy-start.1
  57.9 30.9 %convolution_bitcast_fusion = f32[256,128,256]{0,2,1:T(8,128)} fusion(f32[2,128,256]{2,1,0:T(8,128)S(1)} %all_gather.3, f32[256,2]{0,1:T(2,128)} %param.11), kind=kOutput, calls=%fused_computation | convolution fusion | flops 201326592 | bytes 33818624 | tf_op jit(solution)/shard_map/cp,pab->cab/dot_general | solution.py:21
  88.8 34.1 %copy.17 = f32[256,128,256]{2,1,0:T(8,128)} copy(f32[256,128,256]{0,2,1:T(8,128)} %convolution_bitcast_fusion) | data formatting | bytes 67108864
  122.9 0.0 reduce-scatter.13.cloned.1.call-done
  122.9 0.0 reduce-scatter.7.cloned.1.call-done
  122.9 0.0 copy-done.1
Async XLA Ops:
  7.2 1.2 copy-start
  7.2 18.6 %reduce-scatter.9.cloned.1.call-start = ((), (), s32[]{:S(2)}) async-start(), calls=%async_computation.5 | async-start | bytes 393216 | tf_op jit(solution)/shard_map/reduce_scatter | solution.py:18
  11.2 43.6 %reduce-scatter.11.cloned.1.call-start = ((), (), s32[]{:S(2)}) async-start(), calls=%async_computation.6 | async-start | bytes 655360 | tf_op jit(solution)/shard_map/reduce_scatter | solution.py:20
  28.2 94.7 %reduce-scatter.13.cloned.1.call-start = ((), (), s32[]{:S(2)}) async-start(), calls=%async_computation.7 | async-start | bytes 163840
  31.3 91.6 %reduce-scatter.7.cloned.1.call-start = ((), (), s32[]{:S(2)}) async-start(), calls=%async_computation.4 | async-start | bytes 589824 | tf_op jit(solution)/shard_map/reduce_scatter | solution.py:16
  57.9 65.0 %copy-start.1 = (f32[512,512]{1,0:T(8,128)S(1)}, f32[512,512]{1,0:T(8,128)}, u32[]{:S(2)}) copy-start(f32[512,512]{1,0:T(8,128)} %param.13) | copy-start | bytes 3145732
Sparse Core Ops, SparseCore 0:
  11.4 14.3 reduce-scatter.8
  28.7 21.6 reduce-scatter.10
  53.5 17.8 reduce-scatter.12
  74.2 30.9 reduce-scatter.6
where the time goes:
time: 130 us; the launch traced here: 129 us
  matrix products  40.2 us (31%)
  local copies, waits for them, and re-layouts  37 us (28%)
  blocking collectives  23.1 us (18%)
  waiting for transfers between devices  14.5 us (11%)
  between operations  13.8 us (11%)
    unnamed x6, local copies, waits for them, and re-layouts  36 us
    dot_general x1, matrix products, on_device(): jnp.einsum('cp,pab->cab', core_planes, lax.all_gather(partial_value, 'bz'...  30.9 us
    psum x1, blocking collectives, on_device(): plane_sketch = lax.psum(plane_part, ('bx', 'by'))  21.1 us
    reduce_scatter x1, waiting for transfers between devices, on_device(): reduced = lax.psum_scatter(shrunk, 'by', scatter_dimension=2, tiled=True)  14.5 us
    dot_general x1, matrix products, on_device(): shrunk = jnp.einsum('pij,bj->pib', slab, core_cols, precision=highest)  2.83 us
  transfers between devices with their start and end apart: 4, of which 1 were waited for; matrix products, arithmetic and copies ran while one was open for 55% of the time, Pallas kernels for 0%

commit v1 on v0

v1 whole, which is shorter than its diff:
```python
import functools

import jax
import jax.numpy as jnp
from jax import lax
from jax.experimental import pallas as pl
from jax.experimental.pallas import tpu as pltpu
from jax.sharding import PartitionSpec as P

F32 = jnp.float32
VMEM_LIMIT = 40 << 20
PIECES = (4, 4)


def split(x):
    hi = x.astype(jnp.bfloat16)
    return hi, (x - hi.astype(F32)).astype(jnp.bfloat16)


def dot3(a, b, contract):
    dims = ((contract[:1], contract[1:]), ((), ()))
    (ah, al), (bh, bl) = split(a), split(b)
    dot = functools.partial(lax.dot_general, dimension_numbers=dims, preferred_element_type=F32)
    return dot(ah, bh) + (dot(ah, bl) + dot(al, bh))


def call(kernel, outs, operands, spaces, out_spaces=None, scratch=(), cost=None, **kw):
    vmem = pl.BlockSpec(memory_space=pltpu.VMEM)
    spec = {"v": vmem, "s": pl.BlockSpec(memory_space=pltpu.SMEM), "a": pl.BlockSpec(memory_space=pl.ANY)}
    out_spaces = out_spaces or "v" * len(outs)
    return pl.pallas_call(
        kernel,
        out_shape=[jax.ShapeDtypeStruct(s, F32) for s in outs],
        in_specs=[spec[s] for s in spaces],
        out_specs=[spec[s] for s in out_spaces],
        scratch_shapes=list(scratch),
        cost_estimate=cost and pl.CostEstimate(flops=cost[0], bytes_accessed=cost[1], transcendentals=0),
        compiler_params=pltpu.CompilerParams(vmem_limit_bytes=VMEM_LIMIT),
        **kw,
    )(*operands)


def pairs(n, k):
    return [(i, i ^ k) for i in range(n)]


def shrink_others(n, slab, cols, *refs):
    outs, (s_buf, c_buf, sem) = refs[: n - 1], refs[n - 1 :]
    me = lax.axis_index("by")
    bb = c_buf.shape[1]
    first = pltpu.make_async_copy(slab.at[0], s_buf, sem.at[n - 1])
    first.start()
    copies = []
    for k in range(1, n):
        start = pl.multiple_of((me ^ k) * bb, bb)
        copies.append(pltpu.make_async_copy(cols.at[pl.ds(start, bb)], c_buf.at[k - 1], sem.at[k - 1]))
        copies[-1].start()
    first.wait()
    for k in range(1, n):
        copies[k - 1].wait()
        outs[k - 1][...] = dot3(s_buf[...], c_buf[k - 1], (1, 1))


def local_terms(nbx, nby, nbz, slab, cols, row_test, col_test, plane_test, own, packed, plane, c_buf, sem):
    me = lax.axis_index("by")
    bb = c_buf.shape[0]
    copy = pltpu.make_async_copy(cols.at[pl.ds(pl.multiple_of(me * bb, bb), bb)], c_buf, sem)
    copy.start()
    brick = slab[0]
    nj = brick.shape[1]
    by_row = dot3((row_test[...] * plane_test[...]).T, brick, (1, 0))
    rb = by_row.shape[0] // (nbx * nbz)
    for x in range(nbx):
        for z in range(nbz):
            packed[z, x * rb : (x + 1) * rb, :nj] = by_row[(x * nbz + z) * rb : (x * nbz + z + 1) * rb]
    by_col = dot3(brick, col_test[...], (1, 0))
    total = jnp.sum(by_col * row_test[...], axis=0, keepdims=True)
    plane[...] = jnp.broadcast_to(total, plane.shape)
    by_col = (by_col * plane_test[...]).T
    rb = by_col.shape[0] // (nby * nbz)
    for y in range(nby):
        for z in range(nbz):
            packed[z, y * rb : (y + 1) * rb, nj:] = by_col[(y * nbz + z) * rb : (y * nbz + z + 1) * rb]
    copy.wait()
    own[...] = dot3(brick, c_buf[...], (1, 1))


def core_terms(n, cuts, rows, own, *refs):
    received, outs = refs[: -1 - (n - 1) * (len(cuts) - 1)], refs[-1 - (n - 1) * (len(cuts) - 1) :]
    me = lax.axis_index("bx")
    ab = rows.shape[0] // n
    reduced = own[...]
    for r in received:
        reduced = reduced + r[...]
    hi, lo = split(reduced)
    right = jnp.concatenate([hi, hi, lo], axis=0)

    def block(start, size):
        hi, lo = split(rows[pl.ds(pl.multiple_of(start, 8), size), :])
        left = jnp.concatenate([hi, lo, hi], axis=1)
        return lax.dot_general(left, right, (((1,), (0,)), ((), ())), preferred_element_type=F32)

    at = 1
    for lo_row, hi_row in zip(cuts[:-1], cuts[1:]):
        for k in range(1, n):
            outs[at][...] = block((me ^ k) * ab + lo_row, hi_row - lo_row)
            at += 1
    outs[0][...] = block(me * ab, ab)


def add_all(lo, own, *refs):
    *received, out = refs
    total = own[lo : lo + out.shape[0]]
    for r in received:
        total = total + r[...]
    out[...] = total


def split_sketches(nbx, nby, nj, packed, received, plane, *refs):
    row_own, col_own = refs[0], refs[1]
    row_out, col_out = refs[2 : 1 + nby], refs[1 + nby :]
    z, y, x = lax.axis_index("bz"), lax.axis_index("by"), lax.axis_index("bx")
    rb, cb, ni = row_own.shape[0], col_own.shape[0], row_own.shape[1]

    def row_block(d):
        at = pl.ds(pl.multiple_of(d * rb, 8), rb)
        return packed[z, at, nj:] + received[at, nj:]

    def col_block(d):
        at = pl.ds(pl.multiple_of(d * cb, 8), cb)
        return packed[z, at, :nj] + received[at, :nj]

    row_own[...] = row_block(y)
    col_own[...] = col_block(x)
    for k in range(1, nby):
        row_out[k - 1][:rb] = row_block(y ^ k)
        for part in range(plane.shape[1] // ni):
            row_out[k - 1][rb + 8 * part : rb + 8 * (part + 1)] = plane[:, part * ni : (part + 1) * ni]
    for k in range(1, nbx):
        col_out[k - 1][...] = col_block(x ^ k)


def write_core(at, cb, nb, me, planes, own, other, *refs):
    out, buf, sem = refs[-3:]
    me = lax.axis_index("bz")
    rows = own.shape[0]
    steps = out.shape[0] // cb

    def copy(s, slot):
        return pltpu.make_async_copy(buf.at[slot], out.at[pl.ds(s * cb, cb), pl.ds(at, rows)], sem.at[slot])

    def step(s, _):
        slot = lax.rem(s, nb)

        @pl.when(s >= nb)
        def _():
            copy(s - nb, slot).wait()

        for c in range(cb):
            buf[slot, c] = planes[me, s * cb + c] * own[...] + planes[1 - me, s * cb + c] * other[...]
        copy(s, slot).start()
        return 0

    lax.fori_loop(0, steps, step, 0)

    def drain(s, _):
        copy(s, lax.rem(s, nb)).wait()
        return 0

    lax.fori_loop(steps - nb, steps, drain, 0)


def finish(nbx, nby, plane, *refs):
    row_own, col_own = refs[0], refs[1]
    row_in, col_in, plane_in = refs[2 : 1 + nby], refs[1 + nby : nby + nbx], refs[nby + nbx : nby + 2 * nbx - 1]
    plane_out, row_out, col_out = refs[nby + 2 * nbx - 1 :]
    rb = row_own.shape[0]
    row, col = row_own[...], col_own[...]
    for r in row_in:
        row = row + r[:rb]
    for r in col_in:
        col = col + r[...]
    total = plane[:1]
    for r in plane_in:
        total = total + r[:1]
    plane_out[...] = total
    row_out[...] = row.T
    col_out[...] = col.T


def direct(mesh, slab, plane_test, row_test, col_test, core_planes, core_rows, core_cols):
    nbx, nby, nbz = mesh.shape["bx"], mesh.shape["by"], mesh.shape["bz"]
    _, ni, nj = slab.shape
    k = row_test.shape[1]
    ab, bb = core_rows.shape[0] // nbx, core_cols.shape[0] // nby
    nc = core_planes.shape[0]
    rb, cb = k // (nby * nbz), k // (nbx * nbz)
    cuts = [0]
    for p in PIECES:
        cuts.append(cuts[-1] + p * ab // sum(PIECES))

    outs = call(
        functools.partial(shrink_others, nby),
        [(ni, bb)] * (nby - 1),
        (slab, core_cols),
        "aa",
        scratch=[pltpu.VMEM((ni, nj), F32), pltpu.VMEM((nby - 1, bb, nj), F32), pltpu.SemaphoreType.DMA((nby,))],
        cost=(6 * ni * bb * nj * (nby - 1), 4 * (ni * nj + bb * nj)),
    )
    shrunk_in = [lax.ppermute(o, "by", pairs(nby, i)) for i, o in enumerate(outs, 1)]

    own, packed, plane = call(
        functools.partial(local_terms, nbx, nby, nbz),
        [(ni, bb), (nbz, k // nbz, nj + ni), (8, k)],
        (slab, core_cols, row_test, col_test, plane_test),
        "vavvv",
        scratch=[pltpu.VMEM((bb, nj), F32), pltpu.SemaphoreType.DMA],
        cost=(6 * ni * nj * (bb + 2 * k), 4 * (ni * nj + bb * nj + nj * k)),
    )
    z = lax.axis_index("bz")
    packed_in = lax.ppermute(lax.dynamic_index_in_dim(packed, 1 - z, 0, False), "bz", pairs(nbz, 1))

    outs = call(
        functools.partial(core_terms, nbx, cuts),
        [(ab, bb)] + [(hi - lo, bb) for lo, hi in zip(cuts[:-1], cuts[1:]) for _ in range(nbx - 1)],
        (core_rows, own, *shrunk_in),
        "vv" + "v" * (nby - 1),
        cost=(6 * ni * bb * core_rows.shape[0], 4 * core_rows.size),
    )
    core_own, sends = outs[0], outs[1:]
    arrivals = [
        [lax.ppermute(sends[p * (nbx - 1) + i - 1], "bx", pairs(nbx, i)) for i in range(1, nbx)]
        for p in range(len(PIECES))
    ]

    outs = call(
        functools.partial(split_sketches, nbx, nby, nj),
        [(rb, ni), (cb, nj)] + [(rb + 8 * (k // ni), ni)] * (nby - 1) + [(cb, nj)] * (nbx - 1),
        (packed, packed_in, plane),
        "vvv",
    )
    row_own, col_own, row_send, col_send = outs[0], outs[1], outs[2 : 1 + nby], outs[1 + nby :]
    row_in = [lax.ppermute(o, "by", pairs(nby, i)) for i, o in enumerate(row_send, 1)]
    for r in row_in:
        plane = plane + r[rb:].reshape(k // ni, 8, ni).transpose(1, 0, 2).reshape(8, k)
    plane_in = [lax.ppermute(plane, "bx", pairs(nbx, i)) for i in range(1, nbx)]
    col_in = [lax.ppermute(o, "bx", pairs(nbx, i)) for i, o in enumerate(col_send, 1)]

    planes = core_planes.T
    core = None
    for p, (lo, hi) in enumerate(zip(cuts[:-1], cuts[1:])):
        (total,) = call(
            functools.partial(add_all, lo), [(hi - lo, bb)], (core_own, *arrivals[p]), "v" * nbx
        )
        other = lax.ppermute(total, "bz", pairs(nbz, 1))
        more = {} if core is None else {"input_output_aliases": {3: 0}}
        extra = () if core is None else (core,)
        (core,) = call(
            functools.partial(write_core, lo, 8, 8, None),
            [(nc, ab, bb)],
            (planes, total, other, *extra),
            "svv" + "a" * len(extra),
            "a",
            scratch=[pltpu.VMEM((8, 8, hi - lo, bb), F32), pltpu.SemaphoreType.DMA((8,))],
            cost=(3 * nc * (hi - lo) * bb, 4 * nc * (hi - lo) * bb),
            **more,
        )
    plane_sketch, row_sketch, col_sketch = call(
        functools.partial(finish, nbx, nby),
        [(1, k), (ni, rb), (nj, cb)],
        (plane, row_own, col_own, *row_in, *col_in, *plane_in),
        "v" * (3 + nby - 1 + 2 * (nbx - 1)),
    )
    return plane_sketch, row_sketch, col_sketch, core


def stepwise(slab, plane_test, row_test, col_test, core_planes, core_rows, core_cols):
    einsum = functools.partial(jnp.einsum, precision=lax.Precision.HIGHEST)
    by_col = einsum("pij,jr->pir", slab, col_test)
    plane_part = einsum("pir,ir->pr", by_col, row_test)
    row_part = einsum("pir,pr->ir", by_col, plane_test)
    by_row = einsum("pij,ir->pjr", slab, row_test)
    col_part = einsum("pjr,pr->jr", by_row, plane_test)
    plane_sketch = lax.psum(plane_part, ("bx", "by"))
    row_sketch = lax.psum_scatter(row_part, ("by", "bz"), scatter_dimension=1, tiled=True)
    col_sketch = lax.psum_scatter(col_part, ("bx", "bz"), scatter_dimension=1, tiled=True)
    shrunk = einsum("pij,bj->pib", slab, core_cols)
    reduced = lax.psum_scatter(shrunk, "by", scatter_dimension=2, tiled=True)
    partial_value = einsum("pib,ai->pab", reduced, core_rows)
    partial_value = lax.psum_scatter(partial_value, "bx", scatter_dimension=1, tiled=True)
    both = lax.all_gather(partial_value, "bz", axis=0, tiled=True)
    core_sketch = einsum("cp,pab->cab", core_planes, both)
    return plane_sketch, row_sketch, col_sketch, core_sketch


def solution(mesh):
    in_specs = (
        P(("groups", "bz"), "bx", "by"),
        P("bz", None),
        P("bx", None),
        P("by", None),
        P("bz", None),
        P(None, "bx"),
        P(None, "by"),
    )
    out_specs = (
        P(("groups", "bz"), None),
        P(("groups", "bx"), ("by", "bz")),
        P(("groups", "by"), ("bx", "bz")),
        P(("groups", "bz"), "bx", "by"),
    )
    short = mesh.shape["bx"] in (2, 4) and mesh.shape["by"] in (2, 4) and mesh.shape["bz"] == 2
    body = functools.partial(direct, mesh) if short else stepwise
    return jax.shard_map(body, mesh=mesh, in_specs=in_specs, out_specs=out_specs, check_vma=False)
```

time: 130 us -> 59.4 us (0.46)
  matrix products: 40.2 us -> 0 us
  local copies, waits for them, and re-layouts: 37 us -> 7.89 us
  blocking collectives: 23.1 us -> 0 us
  starting transfers between devices: 0.16 us -> 22.3 us
  Pallas kernels: 0 us -> 15.9 us
  between operations: 13.8 us -> 0.79 us
  waiting for transfers between devices: 14.5 us -> 12.2 us
    dot_general x5 -> x0, matrix products: 40.2 us -> none  [the longest x1 30.9 us: on_device(): jnp.einsum('cp,pab->cab', core_planes, lax.all_gather(partial_value, 'bz'...]
    unnamed x6 -> x16, local copies, waits for them, and re-layouts: 36 us -> 7.86 us
    ppermute x0 -> x17, starting transfers between devices: none -> 22.3 us  [the longest x6 8.88 us: direct(): lax.ppermute(sends[p * (nbx - 1) + i - 1], 'bx', pairs(nbx, i))]
    psum x1 -> x0, blocking collectives: 21.1 us -> none  [on_device(): plane_sketch = lax.psum(plane_part, ('bx', 'by'))]
    pallas_call x0 -> x9, Pallas kernels: none -> 15.9 us  [call(): pl.pallas_call(kernel, out_shape=[jax.ShapeDtypeStruct(s, F32) for s in o...]
    reduce_scatter x3 -> x0, waiting for transfers between devices: 14.5 us -> none  [the longest x1 14.5 us: on_device(): reduced = lax.psum_scatter(shrunk, 'by', scatter_dimension=2, tiled=True)]
    ppermute x0 -> x17, waiting for transfers between devices: none -> 12.2 us  [the longest x6 4.89 us: direct(): lax.ppermute(sends[p * (nbx - 1) + i - 1], 'bx', pairs(nbx, i))]
    all_gather x1 -> x0, blocking collectives: 1.99 us -> none  [on_device(): lax.all_gather(partial_value, 'bz', axis=0, tiled=True)]
  transfers between devices with their start and end apart: 4 -> 17, of which waited for: 1 -> 5; matrix products, arithmetic and copies ran while one was open for 55% -> 0% of each run, Pallas kernels for 0% -> 24%
where the time goes in v1:
time: 59.4 us; the launch traced here: 59 us
  starting transfers between devices  22.3 us (38%)
  Pallas kernels  15.9 us (27%)
  waiting for transfers between devices  12.2 us (21%)
  local copies, waits for them, and re-layouts  7.89 us (13%)
  between operations  0.79 us (1%)
    pallas_call x9, Pallas kernels, call(): pl.pallas_call(kernel, out_shape=[jax.ShapeDtypeStruct(s, F32) for s in o...  15.9 us
    ppermute x6, starting transfers between devices, direct(): lax.ppermute(sends[p * (nbx - 1) + i - 1], 'bx', pairs(nbx, i))  8.88 us
    unnamed x16, local copies, waits for them, and re-layouts  7.86 us
    ppermute x6, waiting for transfers between devices, direct(): lax.ppermute(sends[p * (nbx - 1) + i - 1], 'bx', pairs(nbx, i))  4.89 us
    ppermute x3, starting transfers between devices, direct(): lax.ppermute(o, 'bx', pairs(nbx, i))  4.45 us
    ppermute x3, starting transfers between devices, direct(): plane_in = [lax.ppermute(plane, 'bx', pairs(nbx, i)) for i in range(1, nbx)]  4.27 us
    ppermute x2, waiting for transfers between devices, direct(): lax.ppermute(o, 'by', pairs(nby, i))  4.14 us
    ppermute x2, starting transfers between devices, direct(): lax.ppermute(o, 'by', pairs(nby, i))  4.04 us
  transfers between devices with their start and end apart: 17, of which 5 were waited for; matrix products, arithmetic and copies ran while one was open for 0% of the time, Pallas kernels for 24%

profile of v1, /device:TPU:0, one launch (start us, length us, event | category | flops | bytes accessed | tf_op | source)
XLA Modules:
  0.0 59.0 jit_solution(10172093842876867645)
XLA Ops:
  0.6 1.2 %copy-done = f32[512,512]{1,0:T(8,128)S(1)} copy-done((f32[512,512]{1,0:T(8,128)S(1)}, f32[512,512]{1,0:T(8,128)}, u32[]{:S(2)}) %copy-start) | copy-done | bytes 1048600
  1.9 0.9 %copy-done.1 = f32[1,128,512]{2,1,0:T(8,128)S(1)} copy-done((f32[1,128,512]{2,1,0:T(8,128)S(1)}, f32[1,128,512]{2,1,0:T(8,128)}, u32[]{:S(2)}) %copy-start.1) | copy-done | bytes 262168
  2.8 1.0 %copy-done.2 = f32[512,256]{1,0:T(8,128)S(1)} copy-done((f32[512,256]{1,0:T(8,128)S(1)}, f32[512,256]{1,0:T(8,128)}, u32[]{:S(2)}) %copy-start.2) | copy-done | bytes 524312
  3.9 0.9 %copy-done.4 = f32[128,256]{1,0:T(8,128)S(1)} copy-done((f32[128,256]{1,0:T(8,128)S(1)}, f32[128,256]{1,0:T(8,128)}, u32[]{:S(2)}) %copy-start.4) | copy-done | bytes 131096
  4.8 0.7 %copy-done.6 = f32[1,256]{1,0:T(1,128)S(1)} copy-done((f32[1,256]{1,0:T(1,128)S(1)}, f32[1,256]{1,0:T(1,128)}, u32[]{:S(2)}) %copy-start.6) | copy-done | bytes 1048
  5.4 1.4 %shard_map.102 = (f32[128,256]{1,0:T(8,128)S(1)}, f32[2,128,640]{2,1,0:T(8,128)S(1)}, f32[8,256]{1,0:T(8,128)S(1)}) custom-call(f32[1,128,512]{2,1,0:T(8,128)S(1)} %copy-done.1, f32[512,512]{1,0:T(8,128)S(1)} %copy-done, f32[128,256]{1,0:T(8,128)S(1)} %copy-done.4, f32[512,256]{1,0:T(8,128)S(1)} %copy-done.2, f32[1,256]{1,0:T(1,128)S(1)} %copy-done.6), custom_call_target="tpu_custom_call" | custom-call | flops 301989888 | bytes 1310720 | tf_op jit(solution)/shard_map/pallas_call | solution.py:31
  6.9 0.5 collective-permute-start
  7.4 0.5 shard_map.105
  7.9 2.6 %collective-permute-start.8 = (f32[128,256]{1,0:T(8,128)S(1)}, f32[128,256]{1,0:T(8,128)S(1)}, u32[]{:S(2)}, u32[]{:S(2)}) collective-permute-start(f32[128,256]{1,0:T(8,128)S(1)} %shard_map.105), channel_id=1, source_target_pairs={{0,2},{2,0},{1,3},{3,1},{4,6},{6,4},{5,7},{7,5},{8,10},{10,8},{9,1... | collective-permute-start | bytes 393224 | tf_op jit(solution)/shard_map/ppermute | solution.py:210
  10.4 4.1 %collective-permute-done.8.refs_0_ = f32[128,256]{1,0:T(8,128)S(1)} collective-permute-done((f32[128,256]{1,0:T(8,128)S(1)}, f32[128,256]{1,0:T(8,128)S(1)}, u32[]{:S(2)}, u32[]{:S(2)}) %collective-permute-start.8) | collective-permute-done | bytes 131104 | tf_op jit(solution)/shard_map/ppermute | solution.py:210
  14.6 0.9 %copy-done.3 = f32[512,128]{1,0:T(8,128)S(1)} copy-done((f32[512,128]{1,0:T(8,128)S(1)}, f32[512,128]{1,0:T(8,128)}, u32[]{:S(2)}) %copy-start.3) | copy-done | bytes 262168
  15.5 0.4 shard_map.106
  15.9 1.9 %collective-permute-start.9 = (f32[64,256]{1,0:T(8,128)S(1)}, f32[64,256]{1,0:T(8,128)S(1)}, u32[]{:S(2)}, u32[]{:S(2)}) collective-permute-start(f32[64,256]{1,0:T(8,128)S(1)} %get-tuple-element.36), channel_id=1, source_target_pairs={{0,4},{4,0},{8,12},{12,8},{1,5},{5,1},{9,13},{13,9},{2,6},{6,2},{1... | collective-permute-start | bytes 196616 | tf_op jit(solution)/shard_map/ppermute | solution.py:232
  17.8 2.6 %collective-permute-start.10 = (f32[64,256]{1,0:T(8,128)S(1)}, f32[64,256]{1,0:T(8,128)S(1)}, u32[]{:S(2)}, u32[]{:S(2)}) collective-permute-start(f32[64,256]{1,0:T(8,128)S(1)} %get-tuple-element.37), channel_id=1, source_target_pairs={{0,8},{4,12},{8,0},{12,4},{1,9},{5,13},{9,1},{13,5},{2,10},{6,14},... | collective-permute-start | bytes 196616 | tf_op jit(solution)/shard_map/ppermute | solution.py:232
  20.4 0.0 collective-permute-start.11
  20.4 0.9 %collective-permute-start.13 = (f32[64,256]{1,0:T(8,128)S(1)}, f32[64,256]{1,0:T(8,128)S(1)}, u32[]{:S(2)}, u32[]{:S(2)}) collective-permute-start(f32[64,256]{1,0:T(8,128)S(1)} %get-tuple-element.39), channel_id=1, source_target_pairs={{0,4},{4,0},{8,12},{12,8},{1,5},{5,1},{9,13},{13,9},{2,6},{6,2},{1... | collective-permute-start | bytes 196616 | tf_op jit(solution)/shard_map/ppermute | solution.py:232
  21.3 0.0 collective-permute-done.9.refs_0_
  21.3 3.5 %collective-permute-start.14 = (f32[64,256]{1,0:T(8,128)S(1)}, f32[64,256]{1,0:T(8,128)S(1)}, u32[]{:S(2)}, u32[]{:S(2)}) collective-permute-start(f32[64,256]{1,0:T(8,128)S(1)} %get-tuple-element.40), channel_id=1, source_target_pairs={{0,8},{4,12},{8,0},{12,4},{1,9},{5,13},{9,1},{13,5},{2,10},{6,14},... | collective-permute-start | bytes 196616 | tf_op jit(solution)/shard_map/ppermute | solution.py:232
  24.8 0.0 collective-permute-done.received
  24.8 0.0 collective-permute-start.15
  24.8 0.3 collective-permute-done.10.refs_1_
  25.1 1.5 %collective-permute-start.1 = (f32[80,128]{1,0:T(8,128)S(1)}, f32[80,128]{1,0:T(8,128)S(1)}, u32[]{:S(2)}, u32[]{:S(2)}) collective-permute-start(f32[80,128]{1,0:T(8,128)S(1)} %get-tuple-element.25), channel_id=1, source_target_pairs={{0,2},{2,0},{1,3},{3,1},{4,6},{6,4},{5,7},{7,5},{8,10},{10,8},{9,1... | collective-permute-start | bytes 122888 | tf_op jit(solution)/shard_map/ppermute | solution.py:243
  26.6 0.2 collective-permute-done.11.refs_2_
  26.8 0.1 collective-permute-start.12
  26.9 0.0 collective-permute-done.13.refs_0_
  26.9 4.3 %collective-permute-done.14.refs_1_ = f32[64,256]{1,0:T(8,128)S(1)} collective-permute-done((f32[64,256]{1,0:T(8,128)S(1)}, f32[64,256]{1,0:T(8,128)S(1)}, u32[]{:S(2)}, u32[]{:S(2)}) %collective-permute-start.14) | collective-permute-done | bytes 65568 | tf_op jit(solution)/shard_map/ppermute | solution.py:232
  31.3 0.0 collective-permute-done.15.refs_2_
  31.3 0.1 collective-permute-start.16
  31.4 1.3 %collective-permute-start.2 = (f32[32,512]{1,0:T(8,128)S(1)}, f32[32,512]{1,0:T(8,128)S(1)}, u32[]{:S(2)}, u32[]{:S(2)}) collective-permute-start(f32[32,512]{1,0:T(8,128)S(1)} %get-tuple-element.28), channel_id=1, source_target_pairs={{0,4},{4,0},{8,12},{12,8},{1,5},{5,1},{9,13},{13,9},{2,6},{6,2},{1... | collective-permute-start | bytes 196616 | tf_op jit(solution)/shard_map/ppermute | solution.py:247
  32.7 1.7 %collective-permute-start.3 = (f32[32,512]{1,0:T(8,128)S(1)}, f32[32,512]{1,0:T(8,128)S(1)}, u32[]{:S(2)}, u32[]{:S(2)}) collective-permute-start(f32[32,512]{1,0:T(8,128)S(1)} %get-tuple-element.29), channel_id=1, source_target_pairs={{0,8},{4,12},{8,0},{12,4},{1,9},{5,13},{9,1},{13,5},{2,10},{6,14},... | collective-permute-start | bytes 196616 | tf_op jit(solution)/shard_map/ppermute | solution.py:247
  34.4 0.0 collective-permute-done.1.refs_2_
  34.4 1.4 %collective-permute-start.4 = (f32[32,512]{1,0:T(8,128)S(1)}, f32[32,512]{1,0:T(8,128)S(1)}, u32[]{:S(2)}, u32[]{:S(2)}) collective-permute-start(f32[32,512]{1,0:T(8,128)S(1)} %get-tuple-element.30), channel_id=1, source_target_pairs={{0,12},{4,8},{8,4},{12,0},{1,13},{5,9},{9,5},{13,1},{2,14},{6,10},... | collective-permute-start | bytes 196616 | tf_op jit(solution)/shard_map/ppermute | solution.py:247
  35.8 0.0 collective-permute-done.12.other
  35.8 2.4 %collective-permute-start.7 = (f32[8,256]{1,0:T(8,128)S(1)}, f32[8,256]{1,0:T(8,128)S(1)}, u32[]{:S(2)}, u32[]{:S(2)}) collective-permute-start(f32[8,256]{1,0:T(8,128)S(1)} %fusion.plane), channel_id=1, source_target_pairs={{0,12},{4,8},{8,4},{12,0},{1,13},{5,9},{9,5},{13,1},{2,14},{6,10},... | collective-permute-start | bytes 24584 | tf_op jit(solution)/shard_map/ppermute | solution.py:246
  38.3 0.0 collective-permute-done.16.other
  38.3 0.0 collective-permute-start.6
  38.3 3.1 %collective-permute-done.7.refs_8_ = f32[8,256]{1,0:T(8,128)S(1)} collective-permute-done((f32[8,256]{1,0:T(8,128)S(1)}, f32[8,256]{1,0:T(8,128)S(1)}, u32[]{:S(2)}, u32[]{:S(2)}) %collective-permute-start.7) | collective-permute-done | bytes 8224 | tf_op jit(solution)/shard_map/ppermute | solution.py:246
  41.4 1.8 %collective-permute-start.5 = (f32[8,256]{1,0:T(8,128)S(1)}, f32[8,256]{1,0:T(8,128)S(1)}, u32[]{:S(2)}, u32[]{:S(2)}) collective-permute-start(f32[8,256]{1,0:T(8,128)S(1)} %fusion.plane), channel_id=1, source_target_pairs={{0,4},{4,0},{8,12},{12,8},{1,5},{5,1},{9,13},{13,9},{2,6},{6,2},{1... | collective-permute-start | bytes 24584 | tf_op jit(solution)/shard_map/ppermute | solution.py:246
  43.2 0.7 %copy-done.5 = f32[256,2]{0,1:T(2,128)S(1)} copy-done((f32[256,2]{0,1:T(2,128)S(1)}, f32[256,2]{0,1:T(2,128)}, u32[]{:S(2)}) %copy-start.5) | copy-done | bytes 2072
  43.9 6.5 %shard_map.109.refs_0_ = f32[256,128,256]{2,1,0:T(8,128)} custom-call(f32[2,256]{1,0:T(2,128)S(1)} %bitcast.11, f32[64,256]{1,0:T(8,128)S(1)} %shard_map.108.own, f32[64,256]{1,0:T(8,128)S(1)} %collective-permute-done.16.other), custom_call_target="tpu_custom_call" | custom-call | flops 12582912 | bytes 16777216 | tf_op jit(solution)/shard_map/pallas_call | solution.py:31
  50.4 6.5 %shard_map.110 = f32[256,128,256]{2,1,0:T(8,128)} custom-call(f32[2,256]{1,0:T(2,128)S(1)} %bitcast.12, f32[64,256]{1,0:T(8,128)S(1)} %shard_map.107.own, f32[64,256]{1,0:T(8,128)S(1)} %collective-permute-done.12.other, f32[256,128,256]{2,1,0:T(8,128)} %shard_map.109.refs_0_), custom_call_target="tpu_custom_call", output_to_operand_aliasing={{}: (3, {})} | custom-call | flops 12582912 | bytes 16777216 | tf_op jit(solution)/shard_map/pallas_call | solution.py:31
  56.9 0.0 collective-permute-done.6.refs_7_
  56.9 0.0 collective-permute-done.5.refs_6_
  57.0 0.0 collective-permute-done.2.refs_3_
  57.0 0.0 collective-permute-done.4.refs_5_
  57.0 0.6 %shard_map.104 = (f32[1,256]{1,0:T(1,128)}, f32[128,64]{1,0:T(8,128)S(1)}, f32[512,32]{1,0:T(8,128)S(1)}) custom-call(f32[8,256]{1,0:T(8,128)S(1)} %fusion.plane, f32[64,128]{1,0:T(8,128)S(1)} %get-tuple-element.26.refs_0_, f32[32,512]{1,0:T(8,128)S(1)} %get-tuple-element.27.refs_1_, f32[80,128]{1,0:T(8,128)S(1)} %collective-permute-done.1.refs_2_, ...), custom_call_target="tpu_custom_call" | custom-call | tf_op jit(solution)/shard_map/pallas_call | solution.py:31
  57.6 0.7 %copy.12 = f32[128,64]{0,1:T(8,128)} copy(f32[128,64]{1,0:T(8,128)S(1)} %get-tuple-element.43) | data formatting | bytes 65536
  58.3 0.7 %copy.13 = f32[512,32]{0,1:T(8,128)} copy(f32[512,32]{1,0:T(8,128)S(1)} %get-tuple-element.44) | data formatting | bytes 131072
  (13 shorter events, 0.1 us)
Async XLA Ops:
  0.6 1.2 %copy-start = (f32[512,512]{1,0:T(8,128)S(1)}, f32[512,512]{1,0:T(8,128)}, u32[]{:S(2)}) copy-start(f32[512,512]{1,0:T(8,128)} %cols.3) | copy-start | bytes 3145732
  1.9 0.9 %copy-start.1 = (f32[1,128,512]{2,1,0:T(8,128)S(1)}, f32[1,128,512]{2,1,0:T(8,128)}, u32[]{:S(2)}) copy-start(f32[1,128,512]{2,1,0:T(8,128)} %slab.3) | copy-start | bytes 786436
  2.8 1.0 %copy-start.2 = (f32[512,256]{1,0:T(8,128)S(1)}, f32[512,256]{1,0:T(8,128)}, u32[]{:S(2)}) copy-start(f32[512,256]{1,0:T(8,128)} %col_test.1) | copy-start | bytes 1572868
  3.9 0.9 %copy-start.4 = (f32[128,256]{1,0:T(8,128)S(1)}, f32[128,256]{1,0:T(8,128)}, u32[]{:S(2)}) copy-start(f32[128,256]{1,0:T(8,128)} %row_test.1) | copy-start | bytes 393220
  4.8 0.7 %copy-start.6 = (f32[1,256]{1,0:T(1,128)S(1)}, f32[1,256]{1,0:T(1,128)}, u32[]{:S(2)}) copy-start(f32[1,256]{1,0:T(1,128)} %plane_test.1) | copy-start | bytes 3076
  6.9 17.9 %collective-permute-start = (f32[128,640]{1,0:T(8,128)S(1)}, f32[128,640]{1,0:T(8,128)S(1)}, u32[]{:S(2)}, u32[]{:S(2)}) collective-permute-start(f32[128,640]{1,0:T(8,128)S(1)} %dynamic-slice_bitcast_fusion), channel_id=1, source_target_pairs={{0,1},{1,0},{2,3},{3,2},{4,5},{5,4},{6,7},{7,6},{8,9},{9,8},{10,11... | collective-permute-start | bytes 983048 | tf_op jit(solution)/shard_map/ppermute | solution.py:221
  7.9 6.7 %collective-permute-start.8 = (f32[128,256]{1,0:T(8,128)S(1)}, f32[128,256]{1,0:T(8,128)S(1)}, u32[]{:S(2)}, u32[]{:S(2)}) collective-permute-start(f32[128,256]{1,0:T(8,128)S(1)} %shard_map.105), channel_id=1, source_target_pairs={{0,2},{2,0},{1,3},{3,1},{4,6},{6,4},{5,7},{7,5},{8,10},{10,8},{9,1... | collective-permute-start | bytes 393224 | tf_op jit(solution)/shard_map/ppermute | solution.py:210
  14.6 1.0 %copy-start.3 = (f32[512,128]{1,0:T(8,128)S(1)}, f32[512,128]{1,0:T(8,128)}, u32[]{:S(2)}) copy-start(f32[512,128]{1,0:T(8,128)} %rows.1) | copy-start | bytes 786436
  15.9 5.4 %collective-permute-start.9 = (f32[64,256]{1,0:T(8,128)S(1)}, f32[64,256]{1,0:T(8,128)S(1)}, u32[]{:S(2)}, u32[]{:S(2)}) collective-permute-start(f32[64,256]{1,0:T(8,128)S(1)} %get-tuple-element.36), channel_id=1, source_target_pairs={{0,4},{4,0},{8,12},{12,8},{1,5},{5,1},{9,13},{13,9},{2,6},{6,2},{1... | collective-permute-start | bytes 196616 | tf_op jit(solution)/shard_map/ppermute | solution.py:232
  17.8 7.4 %collective-permute-start.10 = (f32[64,256]{1,0:T(8,128)S(1)}, f32[64,256]{1,0:T(8,128)S(1)}, u32[]{:S(2)}, u32[]{:S(2)}) collective-permute-start(f32[64,256]{1,0:T(8,128)S(1)} %get-tuple-element.37), channel_id=1, source_target_pairs={{0,8},{4,12},{8,0},{12,4},{1,9},{5,13},{9,1},{13,5},{2,10},{6,14},... | collective-permute-start | bytes 196616 | tf_op jit(solution)/shard_map/ppermute | solution.py:232
  20.4 6.4 %collective-permute-start.11 = (f32[64,256]{1,0:T(8,128)S(1)}, f32[64,256]{1,0:T(8,128)S(1)}, u32[]{:S(2)}, u32[]{:S(2)}) collective-permute-start(f32[64,256]{1,0:T(8,128)S(1)} %get-tuple-element.38), channel_id=1, source_target_pairs={{0,12},{4,8},{8,4},{12,0},{1,13},{5,9},{9,5},{13,1},{2,14},{6,10},... | collective-permute-start | bytes 196616 | tf_op jit(solution)/shard_map/ppermute | solution.py:232
  20.4 6.5 %collective-permute-start.13 = (f32[64,256]{1,0:T(8,128)S(1)}, f32[64,256]{1,0:T(8,128)S(1)}, u32[]{:S(2)}, u32[]{:S(2)}) collective-permute-start(f32[64,256]{1,0:T(8,128)S(1)} %get-tuple-element.39), channel_id=1, source_target_pairs={{0,4},{4,0},{8,12},{12,8},{1,5},{5,1},{9,13},{13,9},{2,6},{6,2},{1... | collective-permute-start | bytes 196616 | tf_op jit(solution)/shard_map/ppermute | solution.py:232
  21.3 10.0 %collective-permute-start.14 = (f32[64,256]{1,0:T(8,128)S(1)}, f32[64,256]{1,0:T(8,128)S(1)}, u32[]{:S(2)}, u32[]{:S(2)}) collective-permute-start(f32[64,256]{1,0:T(8,128)S(1)} %get-tuple-element.40), channel_id=1, source_target_pairs={{0,8},{4,12},{8,0},{12,4},{1,9},{5,13},{9,1},{13,5},{2,10},{6,14},... | collective-permute-start | bytes 196616 | tf_op jit(solution)/shard_map/ppermute | solution.py:232
  24.8 6.5 %collective-permute-start.15 = (f32[64,256]{1,0:T(8,128)S(1)}, f32[64,256]{1,0:T(8,128)S(1)}, u32[]{:S(2)}, u32[]{:S(2)}) collective-permute-start(f32[64,256]{1,0:T(8,128)S(1)} %get-tuple-element.41), channel_id=1, source_target_pairs={{0,12},{4,8},{8,4},{12,0},{1,13},{5,9},{9,5},{13,1},{2,14},{6,10},... | collective-permute-start | bytes 196616 | tf_op jit(solution)/shard_map/ppermute | solution.py:232
  25.1 9.3 %collective-permute-start.1 = (f32[80,128]{1,0:T(8,128)S(1)}, f32[80,128]{1,0:T(8,128)S(1)}, u32[]{:S(2)}, u32[]{:S(2)}) collective-permute-start(f32[80,128]{1,0:T(8,128)S(1)} %get-tuple-element.25), channel_id=1, source_target_pairs={{0,2},{2,0},{1,3},{3,1},{4,6},{6,4},{5,7},{7,5},{8,10},{10,8},{9,1... | collective-permute-start | bytes 122888 | tf_op jit(solution)/shard_map/ppermute | solution.py:243
  26.8 9.0 %collective-permute-start.12 = (f32[64,256]{1,0:T(8,128)S(1)}, f32[64,256]{1,0:T(8,128)S(1)}, u32[]{:S(2)}, u32[]{:S(2)}) collective-permute-start(f32[64,256]{1,0:T(8,128)S(1)} %shard_map.107.own), channel_id=1, source_target_pairs={{0,1},{1,0},{2,3},{3,2},{4,5},{5,4},{6,7},{7,6},{8,9},{9,8},{10,11... | collective-permute-start | bytes 196616 | tf_op jit(solution)/shard_map/ppermute | solution.py:255
  31.3 7.0 %collective-permute-start.16 = (f32[64,256]{1,0:T(8,128)S(1)}, f32[64,256]{1,0:T(8,128)S(1)}, u32[]{:S(2)}, u32[]{:S(2)}) collective-permute-start(f32[64,256]{1,0:T(8,128)S(1)} %shard_map.108.own), channel_id=1, source_target_pairs={{0,1},{1,0},{2,3},{3,2},{4,5},{5,4},{6,7},{7,6},{8,9},{9,8},{10,11... | collective-permute-start | bytes 196616 | tf_op jit(solution)/shard_map/ppermute | solution.py:255
  31.4 25.6 %collective-permute-start.2 = (f32[32,512]{1,0:T(8,128)S(1)}, f32[32,512]{1,0:T(8,128)S(1)}, u32[]{:S(2)}, u32[]{:S(2)}) collective-permute-start(f32[32,512]{1,0:T(8,128)S(1)} %get-tuple-element.28), channel_id=1, source_target_pairs={{0,4},{4,0},{8,12},{12,8},{1,5},{5,1},{9,13},{13,9},{2,6},{6,2},{1... | collective-permute-start | bytes 196616 | tf_op jit(solution)/shard_map/ppermute | solution.py:247
  32.7 24.3 %collective-permute-start.3 = (f32[32,512]{1,0:T(8,128)S(1)}, f32[32,512]{1,0:T(8,128)S(1)}, u32[]{:S(2)}, u32[]{:S(2)}) collective-permute-start(f32[32,512]{1,0:T(8,128)S(1)} %get-tuple-element.29), channel_id=1, source_target_pairs={{0,8},{4,12},{8,0},{12,4},{1,9},{5,13},{9,1},{13,5},{2,10},{6,14},... | collective-permute-start | bytes 196616 | tf_op jit(solution)/shard_map/ppermute | solution.py:247
  34.4 22.5 %collective-permute-start.4 = (f32[32,512]{1,0:T(8,128)S(1)}, f32[32,512]{1,0:T(8,128)S(1)}, u32[]{:S(2)}, u32[]{:S(2)}) collective-permute-start(f32[32,512]{1,0:T(8,128)S(1)} %get-tuple-element.30), channel_id=1, source_target_pairs={{0,12},{4,8},{8,4},{12,0},{1,13},{5,9},{9,5},{13,1},{2,14},{6,10},... | collective-permute-start | bytes 196616 | tf_op jit(solution)/shard_map/ppermute | solution.py:247
  35.8 5.6 %collective-permute-start.7 = (f32[8,256]{1,0:T(8,128)S(1)}, f32[8,256]{1,0:T(8,128)S(1)}, u32[]{:S(2)}, u32[]{:S(2)}) collective-permute-start(f32[8,256]{1,0:T(8,128)S(1)} %fusion.plane), channel_id=1, source_target_pairs={{0,12},{4,8},{8,4},{12,0},{1,13},{5,9},{9,5},{13,1},{2,14},{6,10},... | collective-permute-start | bytes 24584 | tf_op jit(solution)/shard_map/ppermute | solution.py:246
  38.3 18.7 %collective-permute-start.6 = (f32[8,256]{1,0:T(8,128)S(1)}, f32[8,256]{1,0:T(8,128)S(1)}, u32[]{:S(2)}, u32[]{:S(2)}) collective-permute-start(f32[8,256]{1,0:T(8,128)S(1)} %fusion.plane), channel_id=1, source_target_pairs={{0,8},{4,12},{8,0},{12,4},{1,9},{5,13},{9,1},{13,5},{2,10},{6,14},... | collective-permute-start | bytes 24584 | tf_op jit(solution)/shard_map/ppermute | solution.py:246
  41.4 15.5 %collective-permute-start.5 = (f32[8,256]{1,0:T(8,128)S(1)}, f32[8,256]{1,0:T(8,128)S(1)}, u32[]{:S(2)}, u32[]{:S(2)}) collective-permute-start(f32[8,256]{1,0:T(8,128)S(1)} %fusion.plane), channel_id=1, source_target_pairs={{0,4},{4,0},{8,12},{12,8},{1,5},{5,1},{9,13},{13,9},{2,6},{6,2},{1... | collective-permute-start | bytes 24584 | tf_op jit(solution)/shard_map/ppermute | solution.py:246
  43.2 0.7 %copy-start.5 = (f32[256,2]{0,1:T(2,128)S(1)}, f32[256,2]{0,1:T(2,128)}, u32[]{:S(2)}) copy-start(f32[256,2]{0,1:T(2,128)} %param.11) | copy-start | bytes 6148

commit v2 on v0

v2 whole, which is shorter than its diff:
```python
import functools

import jax
import jax.numpy as jnp
from jax import lax
from jax.experimental import pallas as pl
from jax.experimental.pallas import tpu as pltpu
from jax.sharding import PartitionSpec as P

F32 = jnp.float32
BF16 = jnp.bfloat16
VMEM_LIMIT = 40 << 20
DIRECT = (4, 2, 2)
FIRST = 5
FIRST_ORDER = (2, 1, 3)
SECOND_ORDER = (1, 2, 3)


def split(x):
    hi = x.astype(BF16)
    return hi, (x - hi.astype(F32)).astype(BF16)


def dot(a, b, contract):
    dims = ((contract[:1], contract[1:]), ((), ()))
    return lax.dot_general(a, b, dims, preferred_element_type=F32)


def rows_dot(a, b):
    m, n = a[0].shape[0], b[0].shape[0]
    r = dot(jnp.concatenate(a), jnp.concatenate(b), (1, 1))
    return r[:m, :n] + (r[:m, n:] + r[m:, :n])


def call(kernel, outs, operands, spaces, out_spaces=None, scratch=(), cost=None, **kw):
    spec = {
        "v": pl.BlockSpec(memory_space=pltpu.VMEM),
        "h": pl.BlockSpec(memory_space=pltpu.HBM),
    }
    out_spaces = out_spaces or "v" * len(outs)
    operands = [
        pltpu.with_memory_space_constraint(o, pltpu.HBM) if s == "h" else o for o, s in zip(operands, spaces)
    ]
    return pl.pallas_call(
        kernel,
        out_shape=[s if hasattr(s, "dtype") else jax.ShapeDtypeStruct(s, F32) for s in outs],
        in_specs=[spec[s] for s in spaces],
        out_specs=[spec[s] for s in out_spaces],
        scratch_shapes=list(scratch),
        cost_estimate=cost and pl.CostEstimate(flops=cost[0], bytes_accessed=cost[1], transcendentals=0),
        compiler_params=pltpu.CompilerParams(vmem_limit_bytes=VMEM_LIMIT),
        **kw,
    )(*operands)


def pairs(n, k):
    return [(i, i ^ k) for i in range(n)]


def block(i, size):
    return pl.ds(pl.multiple_of(i * size, size), size)


def read(sources, buffers, sem):
    copies = [pltpu.make_async_copy(s, b, sem.at[i]) for i, (s, b) in enumerate(zip(sources, buffers))]
    for c in copies:
        c.start()
    return copies


def others_columns(slab, cols, send, s_buf, c_buf, sem):
    other = 1 - lax.axis_index("by")
    bb = send.shape[0]
    copies = read((slab.at[0], cols.at[block(other, bb)]), (s_buf, c_buf), sem)
    copies[0].wait()
    brick = split(s_buf[...])
    copies[1].wait()
    send[...] = rows_dot(split(c_buf[...]), brick)


def own_terms(slab, cols, col_test, row_test, plane_test, core_rows, after, *refs):
    own, row_own, row_away, plane_own, col_own, col_away, left, *bufs, sem = refs
    y, z = lax.axis_index("by"), lax.axis_index("bz")
    s_buf, rt_buf, pt_buf, ct_buf, c_buf, cr_buf = bufs
    bb, ni = own.shape
    copies = read((slab.at[0], row_test, plane_test, col_test, cols.at[block(y, bb)], core_rows), bufs, sem)
    for c in copies[:3]:
        c.wait()
    brick = split(s_buf[...])
    both = jnp.concatenate(brick)
    k = rt_buf.shape[1]
    hi, lo = split((rt_buf[...] * pt_buf[...]).T)
    by_row = dot(jnp.concatenate([jnp.concatenate([hi, hi], axis=1), jnp.concatenate([lo, lo], axis=1)]), both, (1, 0))
    by_row = by_row[:k] + by_row[k:]
    cb = col_own.shape[0] // 4
    for d in range(4):
        at = 2 * d * cb
        low, high = by_row[at : at + cb], by_row[at + cb : at + 2 * cb]
        col_own[d * cb : (d + 1) * cb] = jnp.where(z == 0, low, high)
        col_away[d * cb : (d + 1) * cb] = jnp.where(z == 0, high, low)
    copies[3].wait()
    hi, lo = split(ct_buf[...])
    by_col = dot(both, hi, (1, 0))
    by_col = by_col[:ni] + (by_col[ni:] + dot(brick[0], lo, (1, 0)))
    plane = jnp.sum(by_col * rt_buf[...], axis=0, keepdims=True)
    plane_own[...] = jnp.broadcast_to(plane, plane_own.shape)
    turned = (by_col * pt_buf[...]).T
    rows = row_own.shape[0]
    low, high = turned[:rows], turned[rows:]
    row_own[...] = jnp.where(y == 0, low, high)
    row_away[...] = jnp.where(y == 0, high, low)
    copies[4].wait()
    own[...] = rows_dot(split(c_buf[...]), brick)
    copies[5].wait()
    hi, lo = split(cr_buf[...])
    left[:, :ni] = hi
    left[:, ni : 2 * ni] = lo
    left[:, 2 * ni :] = hi


def core_first(left, own, received, plane, right, *outs):
    x = lax.axis_index("bx")
    ni = own.shape[1]
    hi, lo = split(own[...] + received[...])
    right[:, :ni] = hi
    right[:, ni : 2 * ni] = hi
    right[:, 2 * ni :] = lo
    ab = left.shape[0] // 4
    for k, out in zip(FIRST_ORDER, outs):
        cut = out.shape[0] - 8
        rows = pl.ds(pl.multiple_of((x ^ k) * ab, ab), cut)
        out[:cut] = dot(left[rows], right[...], (1, 1))
        out[cut:] = plane[...]


def core_second(cut, left, right, col_terms, col_received, planes, *refs):
    core_own, col_own, table, *outs, p_buf, sem = refs
    copy = pltpu.make_async_copy(planes, p_buf, sem)
    copy.start()
    x, z = lax.axis_index("bx"), lax.axis_index("bz")
    ab = left.shape[0] // 4
    rest = ab - cut
    cb, wide = col_own.shape[0], core_own.shape[1]
    for k, out in zip(SECOND_ORDER, outs):
        rows = pl.ds(pl.multiple_of((x ^ k) * ab + cut, 16), rest)
        out[:rest] = dot(left[rows], right[...], (1, 1))
        col = col_terms[block(x ^ k, cb)] + col_received[block(x ^ k, cb)]
        for part in range(col.shape[1] // wide):
            out[rest + part * cb : rest + (part + 1) * cb] = col[:, part * wide : (part + 1) * wide]
    col_own[...] = col_terms[block(x, cb)] + col_received[block(x, cb)]
    core_own[...] = dot(left[block(x, ab)], right[...], (1, 1))
    copy.wait()
    for i, p in enumerate((z, 1 - z)):
        table[i] = jnp.broadcast_to(p_buf[pl.ds(p, 1), :], table.shape[:0:-1]).T


def sum_first(core_own, row_away, plane_own, in_a, in_b, in_c, out, x_send, plane_sum):
    cut, rows = out.shape[0], row_away.shape[0]
    ni = row_away.shape[1]
    out[...] = (core_own[:cut] + in_a[:cut]) + (in_b[:cut] + in_c[:cut])
    plane = (plane_own[...] + in_a[cut:]) + (in_b[cut:] + in_c[cut:])
    rows8 = lax.broadcasted_iota(jnp.int32, plane_sum.shape, 0)
    plane = jnp.where(rows8 == 0, plane[:, :ni], plane[:, ni:])
    plane_sum[...] = plane
    x_send[:rows] = row_away[...]
    x_send[rows:] = plane


def sum_second(core_own, row_own, plane_sum, col_own, x_received, in_a, in_b, in_c, core, out, row_mine, plane, col):
    z = lax.axis_index("bz")
    rows, ni = row_own.shape
    rb, cb = rows // 2, col_own.shape[0]
    rest = in_a.shape[0] - col_own.shape[1] // out.shape[1] * cb
    out[:rest] = (core_own[core_own.shape[0] - rest :] + in_a[:rest]) + (in_b[:rest] + in_c[:rest])
    mine, away = block(z, rb), block(1 - z, rb)
    row_mine[...] = row_own[mine] + x_received[mine]
    turned = row_own[away] + x_received[away]
    out[rest:, :ni] = turned[: rb // 2]
    out[rest:, ni:] = turned[rb // 2 :]
    total = plane_sum[...] + x_received[rows:]
    for part in range(plane.shape[1] // ni):
        plane[:, part * ni : (part + 1) * ni] = total[part : part + 1]
    wide = out.shape[1]
    for part in range(col.shape[1] // wide):
        lanes = slice(part * wide, (part + 1) * wide)
        got = slice(rest + part * cb, rest + (part + 1) * cb)
        col[:, lanes] = (col_own[:, lanes] + in_a[got]) + (in_b[got] + in_c[got])


def write(at, own, other, table, out, buf, sem):
    nb, cb, rows = buf.shape[:3]
    steps = out.shape[0] // cb

    def copy(s, slot):
        return pltpu.make_async_copy(buf.at[slot], out.at[block(s, cb), pl.ds(at, rows)], sem.at[slot])

    def step(s, _):
        slot = lax.rem(s, nb)

        @pl.when(s >= nb)
        def _():
            copy(s - nb, slot).wait()

        for c in range(cb):
            row = pl.ds(s * cb + c, 1)
            buf[slot, c] = table[0, row] * own[:rows] + table[1, row] * other[:rows]
        copy(s, slot).start()
        return 0

    lax.fori_loop(0, steps, step, 0)

    def drain(s, _):
        copy(s, lax.rem(s, nb)).wait()
        return 0

    lax.fori_loop(steps - nb, steps, drain, 0)


def write_first(own, other, table, out, buf, sem):
    write(0, own, other, table, out, buf, sem)


def write_second(own, other, table, row_mine, plane, col, core, out, plane_out, row_out, col_out, buf, sem, row_buf, out_sem):
    rest, ni = buf.shape[2], row_buf.shape[1]
    half = row_buf.shape[0] // 2
    row_buf[:half] = row_mine[:half] + other[rest:, :ni]
    row_buf[half:] = row_mine[half:] + other[rest:, ni:]
    copies = read((plane, row_buf, col), (plane_out, row_out, col_out), out_sem)
    write(out.shape[1] - rest, own, other, table, out, buf, sem)
    for c in copies:
        c.wait()


def direct(mesh, slab, plane_test, row_test, col_test, core_planes, core_rows, core_cols):
    nbx, nby, nbz = DIRECT
    _, ni, nj = slab.shape
    k = row_test.shape[1]
    na, nc = core_rows.shape[0], core_planes.shape[0]
    ab, bb = na // nbx, core_cols.shape[0] // nby
    rb, cb = k // (nby * nbz), k // (nbx * nbz)
    cut = FIRST * ab // 8
    rest = ab - cut
    dma = pltpu.SemaphoreType.DMA

    (x_send,) = call(
        others_columns,
        [(bb, ni)],
        (slab, core_cols),
        "hh",
        scratch=[pltpu.VMEM((ni, nj), F32), pltpu.VMEM((bb, nj), F32), dma((2,))],
        cost=(6 * ni * nj * bb, 4 * (ni + bb) * nj),
    )
    x_in = lax.ppermute(x_send, "by", pairs(nby, 1))

    own, row_own, row_away, plane_own, col_terms, col_away, left = call(
        own_terms,
        [
            (bb, ni),
            (nbz * rb, ni),
            (nbz * rb, ni),
            (8, k),
            (nbx * cb, nj),
            (nbx * cb, nj),
            jax.ShapeDtypeStruct((na, 3 * ni), BF16),
        ],
        (slab, core_cols, col_test, row_test, plane_test, core_rows, x_send),
        "hhhhhhv",
        scratch=[
            pltpu.VMEM((ni, nj), F32),
            pltpu.VMEM((ni, k), F32),
            pltpu.VMEM((1, k), F32),
            pltpu.VMEM((nj, k), F32),
            pltpu.VMEM((bb, nj), F32),
            pltpu.VMEM((na, ni), F32),
            dma((6,)),
        ],
        cost=(6 * ni * nj * (bb + 2 * k), 4 * (ni * nj + bb * nj + nj * k)),
    )
    right, *sends = call(
        core_first,
        [jax.ShapeDtypeStruct((bb, 3 * ni), BF16)] + [(cut + 8, bb)] * 3,
        (left, own, x_in, plane_own),
        "vvvv",
        cost=(6 * ni * bb * 3 * cut, 4 * ni * bb),
    )
    col_away, *sends = lax.optimization_barrier((col_away, *sends))
    first_in = [lax.ppermute(s, "bx", pairs(nbx, i)) for i, s in zip(FIRST_ORDER, sends)]
    col_in = lax.ppermute(col_away, "bz", pairs(nbz, 1))

    core_own, col_own, table, *sends = call(
        functools.partial(core_second, cut),
        [(ab, bb), (cb, nj), (2, nc, bb)] + [(rest + cb * nj // bb, bb)] * 3,
        (left, right, col_terms, col_in, core_planes.T),
        "vvvvh",
        scratch=[pltpu.VMEM((nbz, nc), F32), dma],
        cost=(6 * ni * bb * 4 * ab, 4 * ni * bb),
    )
    second_in = [lax.ppermute(s, "bx", pairs(nbx, i)) for i, s in zip(SECOND_ORDER, sends)]

    first, x_send, plane_sum = call(
        sum_first,
        [(cut, bb), (nbz * rb + 8, ni), (8, ni)],
        (core_own, row_away, plane_own, *first_in),
        "vvvvvv",
    )
    first_other = lax.ppermute(first, "bz", pairs(nbz, 1))
    x_in = lax.ppermute(x_send, "by", pairs(nby, 1))
    (core,) = call(
        write_first,
        [(nc, ab, bb)],
        (first, first_other, table),
        "vvv",
        "h",
        scratch=[pltpu.VMEM((8, 8, cut, bb), F32), dma((8,))],
        cost=(3 * nc * cut * bb, 4 * nc * cut * bb),
    )
    second, row_mine, plane, col = call(
        sum_second,
        [(rest + rb // 2, bb), (rb, ni), (1, k), (cb, nj)],
        (core_own, row_own, plane_sum, col_own, x_in, *second_in, core),
        "vvvvvvvvh",
    )
    second_other = lax.ppermute(second, "bz", pairs(nbz, 1))
    core, plane_sketch, row_sketch, col_sketch = call(
        write_second,
        [(nc, ab, bb), (1, k), (rb, ni), (cb, nj)],
        (second, second_other, table, row_mine, plane, col, core),
        "vvvvvvh",
        "hhhh",
        scratch=[pltpu.VMEM((8, 8, rest, bb), F32), dma((8,)), pltpu.VMEM((rb, ni), F32), dma((3,))],
        cost=(3 * nc * rest * bb, 4 * nc * rest * bb),
        input_output_aliases={6: 0},
    )
    return plane_sketch, row_sketch.T, col_sketch.T, core


def stepwise(slab, plane_test, row_test, col_test, core_planes, core_rows, core_cols):
    einsum = functools.partial(jnp.einsum, precision=lax.Precision.HIGHEST)
    by_col = einsum("pij,jr->pir", slab, col_test)
    plane_part = einsum("pir,ir->pr", by_col, row_test)
    row_part = einsum("pir,pr->ir", by_col, plane_test)
    by_row = einsum("pij,ir->pjr", slab, row_test)
    col_part = einsum("pjr,pr->jr", by_row, plane_test)
    plane_sketch = lax.psum(plane_part, ("bx", "by"))
    row_sketch = lax.psum_scatter(row_part, ("by", "bz"), scatter_dimension=1, tiled=True)
    col_sketch = lax.psum_scatter(col_part, ("bx", "bz"), scatter_dimension=1, tiled=True)
    shrunk = einsum("pij,bj->pib", slab, core_cols)
    reduced = lax.psum_scatter(shrunk, "by", scatter_dimension=2, tiled=True)
    partial_value = einsum("pib,ai->pab", reduced, core_rows)
    partial_value = lax.psum_scatter(partial_value, "bx", scatter_dimension=1, tiled=True)
    both = lax.all_gather(partial_value, "bz", axis=0, tiled=True)
    core_sketch = einsum("cp,pab->cab", core_planes, both)
    return plane_sketch, row_sketch, col_sketch, core_sketch


def solution(mesh):
    in_specs = (
        P(("groups", "bz"), "bx", "by"),
        P("bz", None),
        P("bx", None),
        P("by", None),
        P("bz", None),
        P(None, "bx"),
        P(None, "by"),
    )
    out_specs = (
        P(("groups", "bz"), None),
        P(("groups", "bx"), ("by", "bz")),
        P(("groups", "by"), ("bx", "bz")),
        P(("groups", "bz"), "bx", "by"),
    )
    bricks = tuple(mesh.shape[a] for a in ("bx", "by", "bz"))
    body = functools.partial(direct, mesh) if bricks == DIRECT else stepwise
    return jax.shard_map(body, mesh=mesh, in_specs=in_specs, out_specs=out_specs, check_vma=False)
```

time: 130 us -> 36.4 us (0.28)
  matrix products: 40.2 us -> 0 us
  local copies, waits for them, and re-layouts: 37 us -> 0 us
  blocking collectives: 23.1 us -> 0 us
  Pallas kernels: 0 us -> 17 us
  starting transfers between devices: 0.16 us -> 16.2 us
  between operations: 13.8 us -> 0.72 us
  waiting for transfers between devices: 14.5 us -> 2.28 us
    dot_general x5 -> x0, matrix products: 40.2 us -> none  [the longest x1 30.9 us: on_device(): jnp.einsum('cp,pab->cab', core_planes, lax.all_gather(partial_value, 'bz'...]
    unnamed x6 -> x0, local copies, waits for them, and re-layouts: 36 us -> none
    psum x1 -> x0, blocking collectives: 21.1 us -> none  [on_device(): plane_sketch = lax.psum(plane_part, ('bx', 'by'))]
    pallas_call x0 -> x8, Pallas kernels: none -> 17 us  [call(): pl.pallas_call(kernel, out_shape=[s if hasattr(s, 'dtype') else jax.Shape...]
    ppermute x0 -> x11, starting transfers between devices: none -> 16.2 us  [the longest x6 11.3 us: direct(): lax.ppermute(s, 'bx', pairs(nbx, i))]
    reduce_scatter x3 -> x0, waiting for transfers between devices: 14.5 us -> none  [the longest x1 14.5 us: on_device(): reduced = lax.psum_scatter(shrunk, 'by', scatter_dimension=2, tiled=True)]
    ppermute x0 -> x11, waiting for transfers between devices: none -> 2.28 us  [the longest x2 1.14 us: direct(): x_in = lax.ppermute(x_send, 'by', pairs(nby, 1))]
    all_gather x1 -> x0, blocking collectives: 1.99 us -> none  [on_device(): lax.all_gather(partial_value, 'bz', axis=0, tiled=True)]
  transfers between devices with their start and end apart: 4 -> 11, of which waited for: 1 -> 2; matrix products, arithmetic and copies ran while one was open for 55% -> 0% of each run, Pallas kernels for 0% -> 29%
where the time goes in v2:
time: 36.4 us; the launch traced here: 36.2 us
  Pallas kernels  17 us (47%)
  starting transfers between devices  16.2 us (45%)
  waiting for transfers between devices  2.28 us (6%)
  between operations  0.72 us (2%)
    pallas_call x8, Pallas kernels, call(): pl.pallas_call(kernel, out_shape=[s if hasattr(s, 'dtype') else jax.Shape...  17 us
    ppermute x6, starting transfers between devices, direct(): lax.ppermute(s, 'bx', pairs(nbx, i))  11.3 us
    ppermute x2, starting transfers between devices, direct(): x_in = lax.ppermute(x_send, 'by', pairs(nby, 1))  4.55 us
    ppermute x2, waiting for transfers between devices, direct(): x_in = lax.ppermute(x_send, 'by', pairs(nby, 1))  1.14 us
    ppermute x1, waiting for transfers between devices, direct(): second_other = lax.ppermute(second, 'bz', pairs(nbz, 1))  1.11 us
  transfers between devices with their start and end apart: 11, of which 2 were waited for; matrix products, arithmetic and copies ran while one was open for 0% of the time, Pallas kernels for 29%

profile of v2, /device:TPU:0, one launch (start us, length us, event | category | flops | bytes accessed | tf_op | source)
XLA Modules:
  0.0 36.2 jit_solution(2814388065782716334)
XLA Ops:
  0.6 1.5 %shard_map.102.after = f32[256,128]{1,0:T(8,128)S(1)} custom-call(f32[1,128,512]{2,1,0:T(8,128)} %slab.3, f32[512,512]{1,0:T(8,128)} %cols.3), custom_call_target="tpu_custom_call" | custom-call | flops 100663296 | bytes 786432 | tf_op jit(solution)/shard_map/pallas_call | solution.py:44
  2.1 3.0 %collective-permute-start = (f32[256,128]{1,0:T(8,128)S(1)}, f32[256,128]{1,0:T(8,128)S(1)}, u32[]{:S(2)}, u32[]{:S(2)}) collective-permute-start(f32[256,128]{1,0:T(8,128)S(1)} %shard_map.102.after), channel_id=1, source_target_pairs={{0,2},{2,0},{1,3},{3,1},{4,6},{6,4},{5,7},{7,5},{8,10},{10,8},{9,1... | collective-permute-start | bytes 393224 | tf_op jit(solution)/shard_map/ppermute | solution.py:253
  5.1 2.4 %shard_map.103 = (f32[256,128]{1,0:T(8,128)S(1)}, f32[128,128]{1,0:T(8,128)S(1)}, f32[128,128]{1,0:T(8,128)S(1)}, f32[8,256]{1,0:T(8,128)S(1)}, f32[128,512]{1,0...) custom-call(f32[1,128,512]{2,1,0:T(8,128)} %slab.3, f32[512,512]{1,0:T(8,128)} %cols.3, ...), custom_call_target="tpu_custom_call" | custom-call | flops 301989888 | bytes 1310720 | tf_op jit(solution)/shard_map/pallas_call | solution.py:44
  7.5 1.1 %collective-permute-done.received = f32[256,128]{1,0:T(8,128)S(1)} collective-permute-done((f32[256,128]{1,0:T(8,128)S(1)}, f32[256,128]{1,0:T(8,128)S(1)}, u32[]{:S(2)}, u32[]{:S(2)}) %collective-permute-start) | collective-permute-done | bytes 131104 | tf_op jit(solution)/shard_map/ppermute | solution.py:253
  8.6 0.3 shard_map.104
  9.0 0.1 collective-permute-start.1
  9.0 2.9 %collective-permute-start.2 = (f32[88,256]{1,0:T(8,128)S(1)}, f32[88,256]{1,0:T(8,128)S(1)}, u32[]{:S(2)}, u32[]{:S(2)}) collective-permute-start(f32[88,256]{1,0:T(8,128)S(1)} %get-tuple-element.49), channel_id=1, source_target_pairs={{0,8},{4,12},{8,0},{12,4},{1,9},{5,13},{9,1},{13,5},{2,10},{6,14},... | collective-permute-start | bytes 270344 | tf_op jit(solution)/shard_map/ppermute | solution.py:287
  11.9 1.6 %collective-permute-start.3 = (f32[88,256]{1,0:T(8,128)S(1)}, f32[88,256]{1,0:T(8,128)S(1)}, u32[]{:S(2)}, u32[]{:S(2)}) collective-permute-start(f32[88,256]{1,0:T(8,128)S(1)} %get-tuple-element.50), channel_id=1, source_target_pairs={{0,4},{4,0},{8,12},{12,8},{1,5},{5,1},{9,13},{13,9},{2,6},{6,2},{1... | collective-permute-start | bytes 270344 | tf_op jit(solution)/shard_map/ppermute | solution.py:287
  13.5 0.0 collective-permute-start.4
  13.5 0.0 collective-permute-done.1.col_received
  13.5 0.8 %shard_map.105 = (f32[128,256]{1,0:T(8,128)S(1)}, f32[32,512]{1,0:T(8,128)S(1)}, f32[2,256,256]{2,1,0:T(8,128)S(1)}, f32[112,256]{1,0:T(8,128)S(1)}, f32[112,256]{1,0:T(8,128)S(1)}, /*index=5*/f32[112,256]{1,0:T(8,128)S(1)}) custom-call(bf16[512,384]{1,0:T(8,128)(2,1)S(1)} %get-tuple-element.36.left, bf16[256,384]{1,0:T(8,128)(2,1)S(1)} %get-tuple-element.39.right, ...), custom_call_target="tpu_custom_call" | custom-call | flops 100663296 | bytes 131072 | tf_op jit(solution)/shard_map/pallas_call | solution.py:44
  14.4 1.0 %collective-permute-start.6 = (f32[112,256]{1,0:T(8,128)S(1)}, f32[112,256]{1,0:T(8,128)S(1)}, u32[]{:S(2)}, u32[]{:S(2)}) collective-permute-start(f32[112,256]{1,0:T(8,128)S(1)} %get-tuple-element.55), channel_id=1, source_target_pairs={{0,4},{4,0},{8,12},{12,8},{1,5},{5,1},{9,13},{13,9},{2,6},{6,2},{1... | collective-permute-start | bytes 344072 | tf_op jit(solution)/shard_map/ppermute | solution.py:298
  15.3 3.5 %collective-permute-start.7 = (f32[112,256]{1,0:T(8,128)S(1)}, f32[112,256]{1,0:T(8,128)S(1)}, u32[]{:S(2)}, u32[]{:S(2)}) collective-permute-start(f32[112,256]{1,0:T(8,128)S(1)} %get-tuple-element.56), channel_id=1, source_target_pairs={{0,8},{4,12},{8,0},{12,4},{1,9},{5,13},{9,1},{13,5},{2,10},{6,14},... | collective-permute-start | bytes 344072 | tf_op jit(solution)/shard_map/ppermute | solution.py:298
  18.8 0.0 collective-permute-done.2.in_a
  18.8 2.3 %collective-permute-start.8 = (f32[112,256]{1,0:T(8,128)S(1)}, f32[112,256]{1,0:T(8,128)S(1)}, u32[]{:S(2)}, u32[]{:S(2)}) collective-permute-start(f32[112,256]{1,0:T(8,128)S(1)} %get-tuple-element.57), channel_id=1, source_target_pairs={{0,12},{4,8},{8,4},{12,0},{1,13},{5,9},{9,5},{13,1},{2,14},{6,10},... | collective-permute-start | bytes 344072 | tf_op jit(solution)/shard_map/ppermute | solution.py:298
  21.2 0.0 collective-permute-done.3.in_b
  21.2 0.0 collective-permute-done.4.in_c
  21.2 0.1 collective-permute-start.9
  21.3 1.6 %collective-permute-start.5 = (f32[136,128]{1,0:T(8,128)S(1)}, f32[136,128]{1,0:T(8,128)S(1)}, u32[]{:S(2)}, u32[]{:S(2)}) collective-permute-start(f32[136,128]{1,0:T(8,128)S(1)} %get-tuple-element.54), channel_id=1, source_target_pairs={{0,2},{2,0},{1,3},{3,1},{4,6},{6,4},{5,7},{7,5},{8,10},{10,8},{9,1... | collective-permute-start | bytes 208904 | tf_op jit(solution)/shard_map/ppermute | solution.py:307
  22.8 0.0 collective-permute-done.9.other
  22.8 7.2 %shard_map.107.core = f32[256,128,256]{2,1,0:T(8,128)} custom-call(f32[80,256]{1,0:T(8,128)S(1)} %get-tuple-element.58.own, f32[80,256]{1,0:T(8,128)S(1)} %collective-permute-done.9.other, f32[2,256,256]{2,1,0:T(8,128)S(1)} %get-tuple-element.59.table), custom_call_target="tpu_custom_call" | custom-call | flops 15728640 | bytes 20971520 | tf_op jit(solution)/shard_map/pallas_call | solution.py:44
  30.1 0.0 collective-permute-done.5.x_received
  30.1 0.0 collective-permute-done.6.in_a
  30.1 0.0 collective-permute-done.7.in_b
  30.1 0.0 collective-permute-done.8.in_c
  30.1 0.2 collective-permute-start.10
  30.4 1.1 %collective-permute-done.10.other = f32[80,256]{1,0:T(8,128)S(1)} collective-permute-done((f32[80,256]{1,0:T(8,128)S(1)}, f32[80,256]{1,0:T(8,128)S(1)}, u32[]{:S(2)}, u32[]{:S(2)}) %collective-permute-start.10) | collective-permute-done | bytes 81952 | tf_op jit(solution)/shard_map/ppermute | solution.py:323
  31.5 4.7 %shard_map.109 = (f32[256,128,256]{2,1,0:T(8,128)}, f32[1,256]{1,0:T(1,128)}, f32[64,128]{1,0:T(8,128)}, f32[32,512]{1,0:T(8,128)}) custom-call(f32[80,256]{1,0:T(8,128)S(1)} %get-tuple-element.60.own, f32[80,256]{1,0:T(8,128)S(1)} %collective-permute-done.10.other, f32[2,256,256]{2,1,0:T(8,128)S(1)} %get-tuple-element.59.table, ...), custom_call_target="tpu_custom_call", output_to_operand_aliasing={{0}: (6, {})} | custom-call | flops 9437184 | bytes 12582912 | tf_op jit(solution)/shard_map/pallas_call | solution.py:44
  (2 shorter events, 0.1 us)
Async XLA Ops:
  2.1 6.5 %collective-permute-start = (f32[256,128]{1,0:T(8,128)S(1)}, f32[256,128]{1,0:T(8,128)S(1)}, u32[]{:S(2)}, u32[]{:S(2)}) collective-permute-start(f32[256,128]{1,0:T(8,128)S(1)} %shard_map.102.after), channel_id=1, source_target_pairs={{0,2},{2,0},{1,3},{3,1},{4,6},{6,4},{5,7},{7,5},{8,10},{10,8},{9,1... | collective-permute-start | bytes 393224 | tf_op jit(solution)/shard_map/ppermute | solution.py:253
  9.0 4.5 %collective-permute-start.1 = (f32[128,512]{1,0:T(8,128)S(1)}, f32[128,512]{1,0:T(8,128)S(1)}, u32[]{:S(2)}, u32[]{:S(2)}) collective-permute-start(f32[128,512]{1,0:T(8,128)S(1)} %get-tuple-element.45), channel_id=1, source_target_pairs={{0,1},{1,0},{2,3},{3,2},{4,5},{5,4},{6,7},{7,6},{8,9},{9,8},{10,11... | collective-permute-start | bytes 786440 | tf_op jit(solution)/shard_map/ppermute | solution.py:288
  9.0 9.8 %collective-permute-start.2 = (f32[88,256]{1,0:T(8,128)S(1)}, f32[88,256]{1,0:T(8,128)S(1)}, u32[]{:S(2)}, u32[]{:S(2)}) collective-permute-start(f32[88,256]{1,0:T(8,128)S(1)} %get-tuple-element.49), channel_id=1, source_target_pairs={{0,8},{4,12},{8,0},{12,4},{1,9},{5,13},{9,1},{13,5},{2,10},{6,14},... | collective-permute-start | bytes 270344 | tf_op jit(solution)/shard_map/ppermute | solution.py:287
  11.9 9.2 %collective-permute-start.3 = (f32[88,256]{1,0:T(8,128)S(1)}, f32[88,256]{1,0:T(8,128)S(1)}, u32[]{:S(2)}, u32[]{:S(2)}) collective-permute-start(f32[88,256]{1,0:T(8,128)S(1)} %get-tuple-element.50), channel_id=1, source_target_pairs={{0,4},{4,0},{8,12},{12,8},{1,5},{5,1},{9,13},{13,9},{2,6},{6,2},{1... | collective-permute-start | bytes 270344 | tf_op jit(solution)/shard_map/ppermute | solution.py:287
  13.5 7.7 %collective-permute-start.4 = (f32[88,256]{1,0:T(8,128)S(1)}, f32[88,256]{1,0:T(8,128)S(1)}, u32[]{:S(2)}, u32[]{:S(2)}) collective-permute-start(f32[88,256]{1,0:T(8,128)S(1)} %get-tuple-element.51), channel_id=1, source_target_pairs={{0,12},{4,8},{8,4},{12,0},{1,13},{5,9},{9,5},{13,1},{2,14},{6,10},... | collective-permute-start | bytes 270344 | tf_op jit(solution)/shard_map/ppermute | solution.py:287
  14.4 15.7 %collective-permute-start.6 = (f32[112,256]{1,0:T(8,128)S(1)}, f32[112,256]{1,0:T(8,128)S(1)}, u32[]{:S(2)}, u32[]{:S(2)}) collective-permute-start(f32[112,256]{1,0:T(8,128)S(1)} %get-tuple-element.55), channel_id=1, source_target_pairs={{0,4},{4,0},{8,12},{12,8},{1,5},{5,1},{9,13},{13,9},{2,6},{6,2},{1... | collective-permute-start | bytes 344072 | tf_op jit(solution)/shard_map/ppermute | solution.py:298
  15.3 14.8 %collective-permute-start.7 = (f32[112,256]{1,0:T(8,128)S(1)}, f32[112,256]{1,0:T(8,128)S(1)}, u32[]{:S(2)}, u32[]{:S(2)}) collective-permute-start(f32[112,256]{1,0:T(8,128)S(1)} %get-tuple-element.56), channel_id=1, source_target_pairs={{0,8},{4,12},{8,0},{12,4},{1,9},{5,13},{9,1},{13,5},{2,10},{6,14},... | collective-permute-start | bytes 344072 | tf_op jit(solution)/shard_map/ppermute | solution.py:298
  18.8 11.3 %collective-permute-start.8 = (f32[112,256]{1,0:T(8,128)S(1)}, f32[112,256]{1,0:T(8,128)S(1)}, u32[]{:S(2)}, u32[]{:S(2)}) collective-permute-start(f32[112,256]{1,0:T(8,128)S(1)} %get-tuple-element.57), channel_id=1, source_target_pairs={{0,12},{4,8},{8,4},{12,0},{1,13},{5,9},{9,5},{13,1},{2,14},{6,10},... | collective-permute-start | bytes 344072 | tf_op jit(solution)/shard_map/ppermute | solution.py:298
  21.2 1.6 %collective-permute-start.9 = (f32[80,256]{1,0:T(8,128)S(1)}, f32[80,256]{1,0:T(8,128)S(1)}, u32[]{:S(2)}, u32[]{:S(2)}) collective-permute-start(f32[80,256]{1,0:T(8,128)S(1)} %get-tuple-element.58.own), channel_id=1, source_target_pairs={{0,1},{1,0},{2,3},{3,2},{4,5},{5,4},{6,7},{7,6},{8,9},{9,8},{10,11... | collective-permute-start | bytes 245768 | tf_op jit(solution)/shard_map/ppermute | solution.py:306
  21.3 8.8 %collective-permute-start.5 = (f32[136,128]{1,0:T(8,128)S(1)}, f32[136,128]{1,0:T(8,128)S(1)}, u32[]{:S(2)}, u32[]{:S(2)}) collective-permute-start(f32[136,128]{1,0:T(8,128)S(1)} %get-tuple-element.54), channel_id=1, source_target_pairs={{0,2},{2,0},{1,3},{3,1},{4,6},{6,4},{5,7},{7,5},{8,10},{10,8},{9,1... | collective-permute-start | bytes 208904 | tf_op jit(solution)/shard_map/ppermute | solution.py:307
  30.1 1.3 %collective-permute-start.10 = (f32[80,256]{1,0:T(8,128)S(1)}, f32[80,256]{1,0:T(8,128)S(1)}, u32[]{:S(2)}, u32[]{:S(2)}) collective-permute-start(f32[80,256]{1,0:T(8,128)S(1)} %get-tuple-element.60.own), channel_id=1, source_target_pairs={{0,1},{1,0},{2,3},{3,2},{4,5},{5,4},{6,7},{7,6},{8,9},{9,8},{10,11... | collective-permute-start | bytes 245768 | tf_op jit(solution)/shard_map/ppermute | solution.py:323

commit v3 on v2

--- a/solution.py
+++ b/solution.py
@@ -12,6 +12,7 @@
 VMEM_LIMIT = 40 << 20
 DIRECT = (4, 2, 2)
 FIRST = 5
+LAST = 16
 FIRST_ORDER = (2, 1, 3)
 SECOND_ORDER = (1, 2, 3)
 
@@ -78,12 +79,12 @@
     send[...] = rows_dot(split(c_buf[...]), brick)
 
 
-def own_terms(slab, cols, col_test, row_test, plane_test, core_rows, after, *refs):
-    own, row_own, row_away, plane_own, col_own, col_away, left, *bufs, sem = refs
+def own_terms(slab, cols, col_test, row_test, plane_test, core_rows, planes, after, *refs):
+    own, row_own, row_away, plane_own, col_own, col_away, left, table, *bufs, sem = refs
     y, z = lax.axis_index("by"), lax.axis_index("bz")
-    s_buf, rt_buf, pt_buf, ct_buf, c_buf, cr_buf = bufs
+    s_buf, rt_buf, pt_buf, ct_buf, c_buf, cr_buf, p_buf = bufs
     bb, ni = own.shape
-    copies = read((slab.at[0], row_test, plane_test, col_test, cols.at[block(y, bb)], core_rows), bufs, sem)
+    copies = read((slab.at[0], row_test, plane_test, col_test, cols.at[block(y, bb)], core_rows, planes), bufs, sem)
     for c in copies[:3]:
         c.wait()
     brick = split(s_buf[...])
@@ -103,7 +104,8 @@
     by_col = dot(both, hi, (1, 0))
     by_col = by_col[:ni] + (by_col[ni:] + dot(brick[0], lo, (1, 0)))
     plane = jnp.sum(by_col * rt_buf[...], axis=0, keepdims=True)
-    plane_own[...] = jnp.broadcast_to(plane, plane_own.shape)
+    rows8 = lax.broadcasted_iota(jnp.int32, plane_own.shape, 0)
+    plane_own[...] = jnp.where(rows8 == 0, plane[:, :ni], plane[:, ni:])
     turned = (by_col * pt_buf[...]).T
     rows = row_own.shape[0]
     low, high = turned[:rows], turned[rows:]
@@ -116,6 +118,9 @@
     left[:, :ni] = hi
     left[:, ni : 2 * ni] = lo
     left[:, 2 * ni :] = hi
+    copies[6].wait()
+    for i, p in enumerate((z, 1 - z)):
+        table[i] = jnp.broadcast_to(p_buf[pl.ds(p, 1), :], table.shape[:0:-1]).T
 
 
 def core_first(left, own, received, plane, right, *outs):
@@ -127,17 +132,17 @@
     right[:, 2 * ni :] = lo
     ab = left.shape[0] // 4
     for k, out in zip(FIRST_ORDER, outs):
-        cut = out.shape[0] - 8
+        cut = (out.shape[0] - 8) // 2
         rows = pl.ds(pl.multiple_of((x ^ k) * ab, ab), cut)
-        out[:cut] = dot(left[rows], right[...], (1, 1))
-        out[cut:] = plane[...]
-
-
-def core_second(cut, left, right, col_terms, col_received, planes, *refs):
-    core_own, col_own, table, *outs, p_buf, sem = refs
-    copy = pltpu.make_async_copy(planes, p_buf, sem)
-    copy.start()
-    x, z = lax.axis_index("bx"), lax.axis_index("bz")
+        terms = dot(left[rows], right[...], (1, 1))
+        out[:cut] = terms[:, :ni]
+        out[cut : 2 * cut] = terms[:, ni:]
+        out[2 * cut :] = plane[...]
+
+
+def core_second(cut, left, right, col_terms, col_received, *refs):
+    core_own, col_own, *outs = refs
+    x = lax.axis_index("bx")
     ab = left.shape[0] // 4
     rest = ab - cut
     cb, wide = col_own.shape[0], core_own.shape[1]
@@ -149,24 +154,22 @@
             out[rest + part * cb : rest + (part + 1) * cb] = col[:, part * wide : (part + 1) * wide]
     col_own[...] = col_terms[block(x, cb)] + col_received[block(x, cb)]
     core_own[...] = dot(left[block(x, ab)], right[...], (1, 1))
-    copy.wait()
-    for i, p in enumerate((z, 1 - z)):
-        table[i] = jnp.broadcast_to(p_buf[pl.ds(p, 1), :], table.shape[:0:-1]).T
 
 
 def sum_first(core_own, row_away, plane_own, in_a, in_b, in_c, out, x_send, plane_sum):
     cut, rows = out.shape[0], row_away.shape[0]
     ni = row_away.shape[1]
-    out[...] = (core_own[:cut] + in_a[:cut]) + (in_b[:cut] + in_c[:cut])
-    plane = (plane_own[...] + in_a[cut:]) + (in_b[cut:] + in_c[cut:])
-    rows8 = lax.broadcasted_iota(jnp.int32, plane_sum.shape, 0)
-    plane = jnp.where(rows8 == 0, plane[:, :ni], plane[:, ni:])
+    for part in range(2):
+        lanes = slice(part * ni, (part + 1) * ni)
+        got = slice(part * cut, (part + 1) * cut)
+        out[:, lanes] = (core_own[:cut, lanes] + in_a[got]) + (in_b[got] + in_c[got])
+    plane = (plane_own[...] + in_a[2 * cut :]) + (in_b[2 * cut :] + in_c[2 * cut :])
     plane_sum[...] = plane
     x_send[:rows] = row_away[...]
     x_send[rows:] = plane
 
 
-def sum_second(core_own, row_own, plane_sum, col_own, x_received, in_a, in_b, in_c, core, out, row_mine, plane, col):
+def sum_second(core_own, row_own, plane_sum, col_own, x_received, in_a, in_b, in_c, token, out, row_mine, plane, col):
     z = lax.axis_index("bz")
     rows, ni = row_own.shape
     rb, cb = rows // 2, col_own.shape[0]
@@ -187,12 +190,13 @@
         col[:, lanes] = (col_own[:, lanes] + in_a[got]) + (in_b[got] + in_c[got])
 
 
-def write(at, own, other, table, out, buf, sem):
+def write(at, planes, own, other, table, out, buf, sem):
     nb, cb, rows = buf.shape[:3]
-    steps = out.shape[0] // cb
+    start, steps = planes[0] // cb, (planes[1] - planes[0]) // cb
+    nb = min(nb, steps)
 
     def copy(s, slot):
-        return pltpu.make_async_copy(buf.at[slot], out.at[block(s, cb), pl.ds(at, rows)], sem.at[slot])
+        return pltpu.make_async_copy(buf.at[slot], out.at[block(start + s, cb), pl.ds(at, rows)], sem.at[slot])
 
     def step(s, _):
         slot = lax.rem(s, nb)
@@ -202,7 +206,7 @@
             copy(s - nb, slot).wait()
 
         for c in range(cb):
-            row = pl.ds(s * cb + c, 1)
+            row = pl.ds((start + s) * cb + c, 1)
             buf[slot, c] = table[0, row] * own[:rows] + table[1, row] * other[:rows]
         copy(s, slot).start()
         return 0
@@ -216,8 +220,13 @@
     lax.fori_loop(steps - nb, steps, drain, 0)
 
 
-def write_first(own, other, table, out, buf, sem):
-    write(0, own, other, table, out, buf, sem)
+def write_first(own, other, table, out, token, buf, sem):
+    write(0, (0, out.shape[0] - LAST), own, other, table, out, buf, sem)
+    token[...] = jnp.zeros_like(token)
+
+
+def write_rest(own, other, table, core, out, buf, sem):
+    write(0, (out.shape[0] - LAST, out.shape[0]), own, other, table, out, buf, sem)
 
 
 def write_second(own, other, table, row_mine, plane, col, core, out, plane_out, row_out, col_out, buf, sem, row_buf, out_sem):
@@ -226,7 +235,7 @@
     row_buf[:half] = row_mine[:half] + other[rest:, :ni]
     row_buf[half:] = row_mine[half:] + other[rest:, ni:]
     copies = read((plane, row_buf, col), (plane_out, row_out, col_out), out_sem)
-    write(out.shape[1] - rest, own, other, table, out, buf, sem)
+    write(out.shape[1] - rest, (0, out.shape[0]), own, other, table, out, buf, sem)
     for c in copies:
         c.wait()
 
@@ -252,19 +261,20 @@
     )
     x_in = lax.ppermute(x_send, "by", pairs(nby, 1))
 
-    own, row_own, row_away, plane_own, col_terms, col_away, left = call(
+    own, row_own, row_away, plane_own, col_terms, col_away, left, table = call(
         own_terms,
         [
             (bb, ni),
             (nbz * rb, ni),
             (nbz * rb, ni),
-            (8, k),
+            (8, ni),
             (nbx * cb, nj),
             (nbx * cb, nj),
             jax.ShapeDtypeStruct((na, 3 * ni), BF16),
+            (2, nc, bb),
         ],
-        (slab, core_cols, col_test, row_test, plane_test, core_rows, x_send),
-        "hhhhhhv",
+        (slab, core_cols, col_test, row_test, plane_test, core_rows, core_planes.T, x_send),
+        "hhhhhhhv",
         scratch=[
             pltpu.VMEM((ni, nj), F32),
             pltpu.VMEM((ni, k), F32),
@@ -272,13 +282,14 @@
             pltpu.VMEM((nj, k), F32),
             pltpu.VMEM((bb, nj), F32),
             pltpu.VMEM((na, ni), F32),
-            dma((6,)),
+            pltpu.VMEM((nbz, nc), F32),
+            dma((7,)),
         ],
         cost=(6 * ni * nj * (bb + 2 * k), 4 * (ni * nj + bb * nj + nj * k)),
     )
     right, *sends = call(
         core_first,
-        [jax.ShapeDtypeStruct((bb, 3 * ni), BF16)] + [(cut + 8, bb)] * 3,
+        [jax.ShapeDtypeStruct((bb, 3 * ni), BF16)] + [(2 * cut + 8, ni)] * 3,
         (left, own, x_in, plane_own),
         "vvvv",
         cost=(6 * ni * bb * 3 * cut, 4 * ni * bb),
@@ -287,12 +298,11 @@
     first_in = [lax.ppermute(s, "bx", pairs(nbx, i)) for i, s in zip(FIRST_ORDER, sends)]
     col_in = lax.ppermute(col_away, "bz", pairs(nbz, 1))
 
-    core_own, col_own, table, *sends = call(
+    core_own, col_own, *sends = call(
         functools.partial(core_second, cut),
-        [(ab, bb), (cb, nj), (2, nc, bb)] + [(rest + cb * nj // bb, bb)] * 3,
-        (left, right, col_terms, col_in, core_planes.T),
-        "vvvvh",
-        scratch=[pltpu.VMEM((nbz, nc), F32), dma],
+        [(ab, bb), (cb, nj)] + [(rest + cb * nj // bb, bb)] * 3,
+        (left, right, col_terms, col_in),
+        "vvvv",
         cost=(6 * ni * bb * 4 * ab, 4 * ni * bb),
     )
     second_in = [lax.ppermute(s, "bx", pairs(nbx, i)) for i, s in zip(SECOND_ORDER, sends)]
@@ -305,22 +315,33 @@
     )
     first_other = lax.ppermute(first, "bz", pairs(nbz, 1))
     x_in = lax.ppermute(x_send, "by", pairs(nby, 1))
-    (core,) = call(
+    early = nc - LAST
+    core, token = call(
         write_first,
-        [(nc, ab, bb)],
+        [(nc, ab, bb), (8, ni)],
         (first, first_other, table),
         "vvv",
-        "h",
-        scratch=[pltpu.VMEM((8, 8, cut, bb), F32), dma((8,))],
-        cost=(3 * nc * cut * bb, 4 * nc * cut * bb),
+        "hv",
+        scratch=[pltpu.VMEM((16, 4, cut, bb), F32), dma((16,))],
+        cost=(3 * early * cut * bb, 4 * early * cut * bb),
     )
     second, row_mine, plane, col = call(
         sum_second,
         [(rest + rb // 2, bb), (rb, ni), (1, k), (cb, nj)],
-        (core_own, row_own, plane_sum, col_own, x_in, *second_in, core),
-        "vvvvvvvvh",
+        (core_own, row_own, plane_sum, col_own, x_in, *second_in, token),
+        "v" * 9,
     )
     second_other = lax.ppermute(second, "bz", pairs(nbz, 1))
+    (core,) = call(
+        write_rest,
+        [(nc, ab, bb)],
+        (first, first_other, table, core),
+        "vvvh",
+        "h",
+        scratch=[pltpu.VMEM((16, 4, cut, bb), F32), dma((16,))],
+        cost=(3 * LAST * cut * bb, 4 * LAST * cut * bb),
+        input_output_aliases={3: 0},
+    )
     core, plane_sketch, row_sketch, col_sketch = call(
         write_second,
         [(nc, ab, bb), (1, k), (rb, ni), (cb, nj)],

time: 36.4 us -> 35.9 us (0.986)
  waiting for transfers between devices: 2.28 us -> 1.02 us
  Pallas kernels: 17 us -> 17.5 us
    ppermute x1, waiting for transfers between devices: 1.11 us -> 0.01 us  [direct(): second_other = lax.ppermute(second, 'bz', pairs(nbz, 1))]
    pallas_call x8 -> x9, Pallas kernels: 17 us -> 17.5 us  [call(): pl.pallas_call(kernel, out_shape=[s if hasattr(s, 'dtype') else jax.Shape...]
  transfers between devices with their start and end apart: 11 -> 11, of which waited for: 2 -> 1; matrix products, arithmetic and copies ran while one was open for 0% -> 0% of each run, Pallas kernels for 29% -> 31%
where the time goes in v3:
time: 35.9 us; the launch traced here: 35.8 us
  Pallas kernels  17.5 us (49%)
  starting transfers between devices  16.5 us (46%)
  waiting for transfers between devices  1.02 us (3%)
  between operations  0.74 us (2%)
    pallas_call x9, Pallas kernels, call(): pl.pallas_call(kernel, out_shape=[s if hasattr(s, 'dtype') else jax.Shape...  17.5 us
    ppermute x6, starting transfers between devices, direct(): lax.ppermute(s, 'bx', pairs(nbx, i))  11.6 us
    ppermute x2, starting transfers between devices, direct(): x_in = lax.ppermute(x_send, 'by', pairs(nby, 1))  4.55 us
    ppermute x2, waiting for transfers between devices, direct(): x_in = lax.ppermute(x_send, 'by', pairs(nby, 1))  1 us
  transfers between devices with their start and end apart: 11, of which 1 were waited for; matrix products, arithmetic and copies ran while one was open for 0% of the time, Pallas kernels for 31%

profile of v3, /device:TPU:0, one launch (start us, length us, event | category | flops | bytes accessed | tf_op | source)
XLA Modules:
  0.0 35.8 jit_solution(14558059634856000379)
XLA Ops:
  0.6 1.5 %shard_map.102.after = f32[256,128]{1,0:T(8,128)S(1)} custom-call(f32[1,128,512]{2,1,0:T(8,128)} %slab.3, f32[512,512]{1,0:T(8,128)} %cols.3), custom_call_target="tpu_custom_call" | custom-call | flops 100663296 | bytes 786432 | tf_op jit(solution)/shard_map/pallas_call | solution.py:45
  2.1 3.0 %collective-permute-start = (f32[256,128]{1,0:T(8,128)S(1)}, f32[256,128]{1,0:T(8,128)S(1)}, u32[]{:S(2)}, u32[]{:S(2)}) collective-permute-start(f32[256,128]{1,0:T(8,128)S(1)} %shard_map.102.after), channel_id=1, source_target_pairs={{0,2},{2,0},{1,3},{3,1},{4,6},{6,4},{5,7},{7,5},{8,10},{10,8},{9,1... | collective-permute-start | bytes 393224 | tf_op jit(solution)/shard_map/ppermute | solution.py:262
  5.1 2.5 %shard_map.103 = (f32[256,128]{1,0:T(8,128)S(1)}, f32[128,128]{1,0:T(8,128)S(1)}, f32[128,128]{1,0:T(8,128)S(1)}, f32[8,128]{1,0:T(8,128)S(1)}, f32[128,512]{1,0...) custom-call(f32[1,128,512]{2,1,0:T(8,128)} %slab.3, ...), custom_call_target="tpu_custom_call" | custom-call | flops 301989888 | bytes 1310720 | tf_op jit(solution)/shard_map/pallas_call | solution.py:45
  7.6 1.0 %collective-permute-done.received = f32[256,128]{1,0:T(8,128)S(1)} collective-permute-done((f32[256,128]{1,0:T(8,128)S(1)}, f32[256,128]{1,0:T(8,128)S(1)}, u32[]{:S(2)}, u32[]{:S(2)}) %collective-permute-start) | collective-permute-done | bytes 131104 | tf_op jit(solution)/shard_map/ppermute | solution.py:262
  8.6 0.3 shard_map.104
  9.0 0.1 collective-permute-start.1
  9.0 2.9 %collective-permute-start.2 = (f32[168,128]{1,0:T(8,128)S(1)}, f32[168,128]{1,0:T(8,128)S(1)}, u32[]{:S(2)}, u32[]{:S(2)}) collective-permute-start(f32[168,128]{1,0:T(8,128)S(1)} %get-tuple-element.51), channel_id=1, source_target_pairs={{0,8},{4,12},{8,0},{12,4},{1,9},{5,13},{9,1},{13,5},{2,10},{6,14},... | collective-permute-start | bytes 258056 | tf_op jit(solution)/shard_map/ppermute | solution.py:298
  11.9 1.6 %collective-permute-start.3 = (f32[168,128]{1,0:T(8,128)S(1)}, f32[168,128]{1,0:T(8,128)S(1)}, u32[]{:S(2)}, u32[]{:S(2)}) collective-permute-start(f32[168,128]{1,0:T(8,128)S(1)} %get-tuple-element.52), channel_id=1, source_target_pairs={{0,4},{4,0},{8,12},{12,8},{1,5},{5,1},{9,13},{13,9},{2,6},{6,2},{1... | collective-permute-start | bytes 258056 | tf_op jit(solution)/shard_map/ppermute | solution.py:298
  13.5 0.0 collective-permute-start.4
  13.5 0.0 collective-permute-done.1.col_received
  13.5 0.4 %shard_map.105 = (f32[128,256]{1,0:T(8,128)S(1)}, f32[32,512]{1,0:T(8,128)S(1)}, f32[112,256]{1,0:T(8,128)S(1)}, f32[112,256]{1,0:T(8,128)S(1)}, f32[112,256]{1,0:T(8,128)S(1)}) custom-call(bf16[512,384]{1,0:T(8,128)(2,1)S(1)} %get-tuple-element.38.left, bf16[256,384]{1,0:T(8,128)(2,1)S(1)} %get-tuple-element.41.right, ...), custom_call_target="tpu_custom_call" | custom-call | flops 100663296 | bytes 131072 | tf_op jit(solution)/shard_map/pallas_call | solution.py:45
  13.9 1.0 %collective-permute-start.6 = (f32[112,256]{1,0:T(8,128)S(1)}, f32[112,256]{1,0:T(8,128)S(1)}, u32[]{:S(2)}, u32[]{:S(2)}) collective-permute-start(f32[112,256]{1,0:T(8,128)S(1)} %get-tuple-element.57), channel_id=1, source_target_pairs={{0,4},{4,0},{8,12},{12,8},{1,5},{5,1},{9,13},{13,9},{2,6},{6,2},{1... | collective-permute-start | bytes 344072 | tf_op jit(solution)/shard_map/ppermute | solution.py:308
  14.9 3.5 %collective-permute-start.7 = (f32[112,256]{1,0:T(8,128)S(1)}, f32[112,256]{1,0:T(8,128)S(1)}, u32[]{:S(2)}, u32[]{:S(2)}) collective-permute-start(f32[112,256]{1,0:T(8,128)S(1)} %get-tuple-element.58), channel_id=1, source_target_pairs={{0,8},{4,12},{8,0},{12,4},{1,9},{5,13},{9,1},{13,5},{2,10},{6,14},... | collective-permute-start | bytes 344072 | tf_op jit(solution)/shard_map/ppermute | solution.py:308
  18.3 0.0 collective-permute-done.2.in_a
  18.3 2.7 %collective-permute-start.8 = (f32[112,256]{1,0:T(8,128)S(1)}, f32[112,256]{1,0:T(8,128)S(1)}, u32[]{:S(2)}, u32[]{:S(2)}) collective-permute-start(f32[112,256]{1,0:T(8,128)S(1)} %get-tuple-element.59), channel_id=1, source_target_pairs={{0,12},{4,8},{8,4},{12,0},{1,13},{5,9},{9,5},{13,1},{2,14},{6,10},... | collective-permute-start | bytes 344072 | tf_op jit(solution)/shard_map/ppermute | solution.py:308
  21.0 0.0 collective-permute-done.3.in_b
  21.0 0.0 collective-permute-done.4.in_c
  21.0 0.1 collective-permute-start.9
  21.1 1.6 %collective-permute-start.5 = (f32[136,128]{1,0:T(8,128)S(1)}, f32[136,128]{1,0:T(8,128)S(1)}, u32[]{:S(2)}, u32[]{:S(2)}) collective-permute-start(f32[136,128]{1,0:T(8,128)S(1)} %get-tuple-element.56), channel_id=1, source_target_pairs={{0,2},{2,0},{1,3},{3,1},{4,6},{6,4},{5,7},{7,5},{8,10},{10,8},{9,1... | collective-permute-start | bytes 208904 | tf_op jit(solution)/shard_map/ppermute | solution.py:317
  22.7 0.0 collective-permute-done.9.other
  22.7 6.8 %shard_map.107 = (f32[256,128,256]{2,1,0:T(8,128)}, f32[8,128]{1,0:T(8,128)S(1)}) custom-call(f32[80,256]{1,0:T(8,128)S(1)} %get-tuple-element.60.own, f32[80,256]{1,0:T(8,128)S(1)} %collective-permute-done.9.other, f32[2,256,256]{2,1,0:T(8,128)S(1)} %get-tuple-element.61.table), custom_call_target="tpu_custom_call" | custom-call | flops 14745600 | bytes 19660800 | tf_op jit(solution)/shard_map/pallas_call | solution.py:45
  29.5 0.0 collective-permute-done.5.x_received
  29.5 0.0 collective-permute-done.6.in_a
  29.6 0.0 collective-permute-done.7.in_b
  29.6 0.0 collective-permute-done.8.in_c
  29.6 0.2 collective-permute-start.10
  29.8 1.2 %shard_map.109.core = f32[256,128,256]{2,1,0:T(8,128)} custom-call(f32[80,256]{1,0:T(8,128)S(1)} %get-tuple-element.60.own, f32[80,256]{1,0:T(8,128)S(1)} %collective-permute-done.9.other, f32[2,256,256]{2,1,0:T(8,128)S(1)} %get-tuple-element.61.table, f32[256,128,256]{2,1,0:T(8,128)} %get-tuple-element.67.core), custom_call_target="tpu_custom_call", output_to_operand_aliasing={{}: (3, {})} | custom-call | flops 983040 | bytes 1310720 | tf_op jit(solution)/shard_map/pallas_call | solution.py:45
  31.1 0.0 collective-permute-done.10.other
  31.1 4.7 %shard_map.110 = (f32[256,128,256]{2,1,0:T(8,128)}, f32[1,256]{1,0:T(1,128)}, f32[64,128]{1,0:T(8,128)}, f32[32,512]{1,0:T(8,128)}) custom-call(f32[80,256]{1,0:T(8,128)S(1)} %get-tuple-element.63.own, f32[80,256]{1,0:T(8,128)S(1)} %collective-permute-done.10.other, f32[2,256,256]{2,1,0:T(8,128)S(1)} %get-tuple-element.61.table, ...), custom_call_target="tpu_custom_call", output_to_operand_aliasing={{0}: (6, {})} | custom-call | flops 9437184 | bytes 12582912 | tf_op jit(solution)/shard_map/pallas_call | solution.py:45
  (2 shorter events, 0.1 us)
Async XLA Ops:
  2.1 6.5 %collective-permute-start = (f32[256,128]{1,0:T(8,128)S(1)}, f32[256,128]{1,0:T(8,128)S(1)}, u32[]{:S(2)}, u32[]{:S(2)}) collective-permute-start(f32[256,128]{1,0:T(8,128)S(1)} %shard_map.102.after), channel_id=1, source_target_pairs={{0,2},{2,0},{1,3},{3,1},{4,6},{6,4},{5,7},{7,5},{8,10},{10,8},{9,1... | collective-permute-start | bytes 393224 | tf_op jit(solution)/shard_map/ppermute | solution.py:262
  9.0 4.5 %collective-permute-start.1 = (f32[128,512]{1,0:T(8,128)S(1)}, f32[128,512]{1,0:T(8,128)S(1)}, u32[]{:S(2)}, u32[]{:S(2)}) collective-permute-start(f32[128,512]{1,0:T(8,128)S(1)} %get-tuple-element.47), channel_id=1, source_target_pairs={{0,1},{1,0},{2,3},{3,2},{4,5},{5,4},{6,7},{7,6},{8,9},{9,8},{10,11... | collective-permute-start | bytes 786440 | tf_op jit(solution)/shard_map/ppermute | solution.py:299
  9.0 9.3 %collective-permute-start.2 = (f32[168,128]{1,0:T(8,128)S(1)}, f32[168,128]{1,0:T(8,128)S(1)}, u32[]{:S(2)}, u32[]{:S(2)}) collective-permute-start(f32[168,128]{1,0:T(8,128)S(1)} %get-tuple-element.51), channel_id=1, source_target_pairs={{0,8},{4,12},{8,0},{12,4},{1,9},{5,13},{9,1},{13,5},{2,10},{6,14},... | collective-permute-start | bytes 258056 | tf_op jit(solution)/shard_map/ppermute | solution.py:298
  11.9 9.1 %collective-permute-start.3 = (f32[168,128]{1,0:T(8,128)S(1)}, f32[168,128]{1,0:T(8,128)S(1)}, u32[]{:S(2)}, u32[]{:S(2)}) collective-permute-start(f32[168,128]{1,0:T(8,128)S(1)} %get-tuple-element.52), channel_id=1, source_target_pairs={{0,4},{4,0},{8,12},{12,8},{1,5},{5,1},{9,13},{13,9},{2,6},{6,2},{1... | collective-permute-start | bytes 258056 | tf_op jit(solution)/shard_map/ppermute | solution.py:298
  13.5 7.5 %collective-permute-start.4 = (f32[168,128]{1,0:T(8,128)S(1)}, f32[168,128]{1,0:T(8,128)S(1)}, u32[]{:S(2)}, u32[]{:S(2)}) collective-permute-start(f32[168,128]{1,0:T(8,128)S(1)} %get-tuple-element.53), channel_id=1, source_target_pairs={{0,12},{4,8},{8,4},{12,0},{1,13},{5,9},{9,5},{13,1},{2,14},{6,10},... | collective-permute-start | bytes 258056 | tf_op jit(solution)/shard_map/ppermute | solution.py:298
  13.9 15.7 %collective-permute-start.6 = (f32[112,256]{1,0:T(8,128)S(1)}, f32[112,256]{1,0:T(8,128)S(1)}, u32[]{:S(2)}, u32[]{:S(2)}) collective-permute-start(f32[112,256]{1,0:T(8,128)S(1)} %get-tuple-element.57), channel_id=1, source_target_pairs={{0,4},{4,0},{8,12},{12,8},{1,5},{5,1},{9,13},{13,9},{2,6},{6,2},{1... | collective-permute-start | bytes 344072 | tf_op jit(solution)/shard_map/ppermute | solution.py:308
  14.9 14.7 %collective-permute-start.7 = (f32[112,256]{1,0:T(8,128)S(1)}, f32[112,256]{1,0:T(8,128)S(1)}, u32[]{:S(2)}, u32[]{:S(2)}) collective-permute-start(f32[112,256]{1,0:T(8,128)S(1)} %get-tuple-element.58), channel_id=1, source_target_pairs={{0,8},{4,12},{8,0},{12,4},{1,9},{5,13},{9,1},{13,5},{2,10},{6,14},... | collective-permute-start | bytes 344072 | tf_op jit(solution)/shard_map/ppermute | solution.py:308
  18.3 11.2 %collective-permute-start.8 = (f32[112,256]{1,0:T(8,128)S(1)}, f32[112,256]{1,0:T(8,128)S(1)}, u32[]{:S(2)}, u32[]{:S(2)}) collective-permute-start(f32[112,256]{1,0:T(8,128)S(1)} %get-tuple-element.59), channel_id=1, source_target_pairs={{0,12},{4,8},{8,4},{12,0},{1,13},{5,9},{9,5},{13,1},{2,14},{6,10},... | collective-permute-start | bytes 344072 | tf_op jit(solution)/shard_map/ppermute | solution.py:308
  21.0 1.6 %collective-permute-start.9 = (f32[80,256]{1,0:T(8,128)S(1)}, f32[80,256]{1,0:T(8,128)S(1)}, u32[]{:S(2)}, u32[]{:S(2)}) collective-permute-start(f32[80,256]{1,0:T(8,128)S(1)} %get-tuple-element.60.own), channel_id=1, source_target_pairs={{0,1},{1,0},{2,3},{3,2},{4,5},{5,4},{6,7},{7,6},{8,9},{9,8},{10,11... | collective-permute-start | bytes 245768 | tf_op jit(solution)/shard_map/ppermute | solution.py:316
  21.1 8.4 %collective-permute-start.5 = (f32[136,128]{1,0:T(8,128)S(1)}, f32[136,128]{1,0:T(8,128)S(1)}, u32[]{:S(2)}, u32[]{:S(2)}) collective-permute-start(f32[136,128]{1,0:T(8,128)S(1)} %get-tuple-element.56), channel_id=1, source_target_pairs={{0,2},{2,0},{1,3},{3,1},{4,6},{6,4},{5,7},{7,5},{8,10},{10,8},{9,1... | collective-permute-start | bytes 208904 | tf_op jit(solution)/shard_map/ppermute | solution.py:317
  29.6 1.5 %collective-permute-start.10 = (f32[80,256]{1,0:T(8,128)S(1)}, f32[80,256]{1,0:T(8,128)S(1)}, u32[]{:S(2)}, u32[]{:S(2)}) collective-permute-start(f32[80,256]{1,0:T(8,128)S(1)} %get-tuple-element.63.own), channel_id=1, source_target_pairs={{0,1},{1,0},{2,3},{3,2},{4,5},{5,4},{6,7},{7,6},{8,9},{9,8},{10,11... | collective-permute-start | bytes 245768 | tf_op jit(solution)/shard_map/ppermute | solution.py:334

commit v4 on v3

--- a/solution.py
+++ b/solution.py
@@ -131,10 +131,11 @@
     right[:, ni : 2 * ni] = hi
     right[:, 2 * ni :] = lo
     ab = left.shape[0] // 4
-    for k, out in zip(FIRST_ORDER, outs):
-        cut = (out.shape[0] - 8) // 2
-        rows = pl.ds(pl.multiple_of((x ^ k) * ab, ab), cut)
-        terms = dot(left[rows], right[...], (1, 1))
+    cut = (outs[0].shape[0] - 8) // 2
+    rows = [left[pl.ds(pl.multiple_of((x ^ k) * ab, ab), cut)] for k in FIRST_ORDER]
+    stacked = dot(jnp.concatenate(rows), right[...], (1, 1))
+    for i, out in enumerate(outs):
+        terms = stacked[i * cut : (i + 1) * cut]
         out[:cut] = terms[:, :ni]
         out[cut : 2 * cut] = terms[:, ni:]
         out[2 * cut :] = plane[...]
@@ -146,14 +147,15 @@
     ab = left.shape[0] // 4
     rest = ab - cut
     cb, wide = col_own.shape[0], core_own.shape[1]
-    for k, out in zip(SECOND_ORDER, outs):
-        rows = pl.ds(pl.multiple_of((x ^ k) * ab + cut, 16), rest)
-        out[:rest] = dot(left[rows], right[...], (1, 1))
+    rows = [left[pl.ds(pl.multiple_of((x ^ k) * ab + cut, 16), rest)] for k in SECOND_ORDER]
+    stacked = dot(jnp.concatenate([*rows, left[block(x, ab)]]), right[...], (1, 1))
+    core_own[...] = stacked[3 * rest :]
+    for i, (k, out) in enumerate(zip(SECOND_ORDER, outs)):
+        out[:rest] = stacked[i * rest : (i + 1) * rest]
         col = col_terms[block(x ^ k, cb)] + col_received[block(x ^ k, cb)]
         for part in range(col.shape[1] // wide):
             out[rest + part * cb : rest + (part + 1) * cb] = col[:, part * wide : (part + 1) * wide]
     col_own[...] = col_terms[block(x, cb)] + col_received[block(x, cb)]
-    core_own[...] = dot(left[block(x, ab)], right[...], (1, 1))
 
 
 def sum_first(core_own, row_away, plane_own, in_a, in_b, in_c, out, x_send, plane_sum):

time: 35.9 us -> 35.9 us (level)
  transfers between devices with their start and end apart: 11 -> 11, of which waited for: 1 -> 1; matrix products, arithmetic and copies ran while one was open for 0% -> 0% of each run, Pallas kernels for 31% -> 30%
where the time goes in v4:
time: 35.9 us; the launch traced here: 35.7 us
  Pallas kernels  17.3 us (48%)
  starting transfers between devices  16.6 us (46%)
  waiting for transfers between devices  1.02 us (3%)
  between operations  0.75 us (2%)
    pallas_call x9, Pallas kernels, call(): pl.pallas_call(kernel, out_shape=[s if hasattr(s, 'dtype') else jax.Shape...  17.3 us
    ppermute x6, starting transfers between devices, direct(): lax.ppermute(s, 'bx', pairs(nbx, i))  11.7 us
    ppermute x2, starting transfers between devices, direct(): x_in = lax.ppermute(x_send, 'by', pairs(nby, 1))  4.55 us
    ppermute x2, waiting for transfers between devices, direct(): x_in = lax.ppermute(x_send, 'by', pairs(nby, 1))  1 us
  transfers between devices with their start and end apart: 11, of which 1 were waited for; matrix products, arithmetic and copies ran while one was open for 0% of the time, Pallas kernels for 30%

profile of v4, /device:TPU:0, one launch (start us, length us, event | category | flops | bytes accessed | tf_op | source)
XLA Modules:
  0.0 35.7 jit_solution(6278217470922947025)
XLA Ops:
  0.6 1.5 %shard_map.102.after = f32[256,128]{1,0:T(8,128)S(1)} custom-call(f32[1,128,512]{2,1,0:T(8,128)} %slab.3, f32[512,512]{1,0:T(8,128)} %cols.3), custom_call_target="tpu_custom_call" | custom-call | flops 100663296 | bytes 786432 | tf_op jit(solution)/shard_map/pallas_call | solution.py:45
  2.1 3.0 %collective-permute-start = (f32[256,128]{1,0:T(8,128)S(1)}, f32[256,128]{1,0:T(8,128)S(1)}, u32[]{:S(2)}, u32[]{:S(2)}) collective-permute-start(f32[256,128]{1,0:T(8,128)S(1)} %shard_map.102.after), channel_id=1, source_target_pairs={{0,2},{2,0},{1,3},{3,1},{4,6},{6,4},{5,7},{7,5},{8,10},{10,8},{9,1... | collective-permute-start | bytes 393224 | tf_op jit(solution)/shard_map/ppermute | solution.py:264
  5.1 2.5 %shard_map.103 = (f32[256,128]{1,0:T(8,128)S(1)}, f32[128,128]{1,0:T(8,128)S(1)}, f32[128,128]{1,0:T(8,128)S(1)}, f32[8,128]{1,0:T(8,128)S(1)}, f32[128,512]{1,0...) custom-call(f32[1,128,512]{2,1,0:T(8,128)} %slab.3, ...), custom_call_target="tpu_custom_call" | custom-call | flops 301989888 | bytes 1310720 | tf_op jit(solution)/shard_map/pallas_call | solution.py:45
  7.6 1.0 %collective-permute-done.received = f32[256,128]{1,0:T(8,128)S(1)} collective-permute-done((f32[256,128]{1,0:T(8,128)S(1)}, f32[256,128]{1,0:T(8,128)S(1)}, u32[]{:S(2)}, u32[]{:S(2)}) %collective-permute-start) | collective-permute-done | bytes 131104 | tf_op jit(solution)/shard_map/ppermute | solution.py:264
  8.6 0.3 shard_map.104
  8.9 0.1 collective-permute-start.1
  9.0 2.9 %collective-permute-start.2 = (f32[168,128]{1,0:T(8,128)S(1)}, f32[168,128]{1,0:T(8,128)S(1)}, u32[]{:S(2)}, u32[]{:S(2)}) collective-permute-start(f32[168,128]{1,0:T(8,128)S(1)} %get-tuple-element.51), channel_id=1, source_target_pairs={{0,8},{4,12},{8,0},{12,4},{1,9},{5,13},{9,1},{13,5},{2,10},{6,14},... | collective-permute-start | bytes 258056 | tf_op jit(solution)/shard_map/ppermute | solution.py:300
  11.9 1.6 %collective-permute-start.3 = (f32[168,128]{1,0:T(8,128)S(1)}, f32[168,128]{1,0:T(8,128)S(1)}, u32[]{:S(2)}, u32[]{:S(2)}) collective-permute-start(f32[168,128]{1,0:T(8,128)S(1)} %get-tuple-element.52), channel_id=1, source_target_pairs={{0,4},{4,0},{8,12},{12,8},{1,5},{5,1},{9,13},{13,9},{2,6},{6,2},{1... | collective-permute-start | bytes 258056 | tf_op jit(solution)/shard_map/ppermute | solution.py:300
  13.4 0.0 collective-permute-start.4
  13.4 0.0 collective-permute-done.1.col_received
  13.4 0.3 shard_map.105
  13.7 1.0 %collective-permute-start.6 = (f32[112,256]{1,0:T(8,128)S(1)}, f32[112,256]{1,0:T(8,128)S(1)}, u32[]{:S(2)}, u32[]{:S(2)}) collective-permute-start(f32[112,256]{1,0:T(8,128)S(1)} %get-tuple-element.57), channel_id=1, source_target_pairs={{0,4},{4,0},{8,12},{12,8},{1,5},{5,1},{9,13},{13,9},{2,6},{6,2},{1... | collective-permute-start | bytes 344072 | tf_op jit(solution)/shard_map/ppermute | solution.py:310
  14.7 3.5 %collective-permute-start.7 = (f32[112,256]{1,0:T(8,128)S(1)}, f32[112,256]{1,0:T(8,128)S(1)}, u32[]{:S(2)}, u32[]{:S(2)}) collective-permute-start(f32[112,256]{1,0:T(8,128)S(1)} %get-tuple-element.58), channel_id=1, source_target_pairs={{0,8},{4,12},{8,0},{12,4},{1,9},{5,13},{9,1},{13,5},{2,10},{6,14},... | collective-permute-start | bytes 344072 | tf_op jit(solution)/shard_map/ppermute | solution.py:310
  18.2 0.0 collective-permute-done.2.in_a
  18.2 2.8 %collective-permute-start.8 = (f32[112,256]{1,0:T(8,128)S(1)}, f32[112,256]{1,0:T(8,128)S(1)}, u32[]{:S(2)}, u32[]{:S(2)}) collective-permute-start(f32[112,256]{1,0:T(8,128)S(1)} %get-tuple-element.59), channel_id=1, source_target_pairs={{0,12},{4,8},{8,4},{12,0},{1,13},{5,9},{9,5},{13,1},{2,14},{6,10},... | collective-permute-start | bytes 344072 | tf_op jit(solution)/shard_map/ppermute | solution.py:310
  21.0 0.0 collective-permute-done.3.in_b
  21.0 0.0 collective-permute-done.4.in_c
  21.0 0.1 collective-permute-start.9
  21.1 1.6 %collective-permute-start.5 = (f32[136,128]{1,0:T(8,128)S(1)}, f32[136,128]{1,0:T(8,128)S(1)}, u32[]{:S(2)}, u32[]{:S(2)}) collective-permute-start(f32[136,128]{1,0:T(8,128)S(1)} %get-tuple-element.56), channel_id=1, source_target_pairs={{0,2},{2,0},{1,3},{3,1},{4,6},{6,4},{5,7},{7,5},{8,10},{10,8},{9,1... | collective-permute-start | bytes 208904 | tf_op jit(solution)/shard_map/ppermute | solution.py:319
  22.6 0.0 collective-permute-done.9.other
  22.6 6.8 %shard_map.107 = (f32[256,128,256]{2,1,0:T(8,128)}, f32[8,128]{1,0:T(8,128)S(1)}) custom-call(f32[80,256]{1,0:T(8,128)S(1)} %get-tuple-element.60.own, f32[80,256]{1,0:T(8,128)S(1)} %collective-permute-done.9.other, f32[2,256,256]{2,1,0:T(8,128)S(1)} %get-tuple-element.61.table), custom_call_target="tpu_custom_call" | custom-call | flops 14745600 | bytes 19660800 | tf_op jit(solution)/shard_map/pallas_call | solution.py:45
  29.5 0.0 collective-permute-done.5.x_received
  29.5 0.0 collective-permute-done.6.in_a
  29.5 0.0 collective-permute-done.7.in_b
  29.5 0.0 collective-permute-done.8.in_c
  29.6 0.2 collective-permute-start.10
  29.8 1.2 %shard_map.109.core = f32[256,128,256]{2,1,0:T(8,128)} custom-call(f32[80,256]{1,0:T(8,128)S(1)} %get-tuple-element.60.own, f32[80,256]{1,0:T(8,128)S(1)} %collective-permute-done.9.other, f32[2,256,256]{2,1,0:T(8,128)S(1)} %get-tuple-element.61.table, f32[256,128,256]{2,1,0:T(8,128)} %get-tuple-element.67.core), custom_call_target="tpu_custom_call", output_to_operand_aliasing={{}: (3, {})} | custom-call | flops 983040 | bytes 1310720 | tf_op jit(solution)/shard_map/pallas_call | solution.py:45
  31.0 0.0 collective-permute-done.10.other
  31.0 4.7 %shard_map.110 = (f32[256,128,256]{2,1,0:T(8,128)}, f32[1,256]{1,0:T(1,128)}, f32[64,128]{1,0:T(8,128)}, f32[32,512]{1,0:T(8,128)}) custom-call(f32[80,256]{1,0:T(8,128)S(1)} %get-tuple-element.63.own, f32[80,256]{1,0:T(8,128)S(1)} %collective-permute-done.10.other, f32[2,256,256]{2,1,0:T(8,128)S(1)} %get-tuple-element.61.table, ...), custom_call_target="tpu_custom_call", output_to_operand_aliasing={{0}: (6, {})} | custom-call | flops 9437184 | bytes 12582912 | tf_op jit(solution)/shard_map/pallas_call | solution.py:45
  (2 shorter events, 0.1 us)
Async XLA Ops:
  2.1 6.5 %collective-permute-start = (f32[256,128]{1,0:T(8,128)S(1)}, f32[256,128]{1,0:T(8,128)S(1)}, u32[]{:S(2)}, u32[]{:S(2)}) collective-permute-start(f32[256,128]{1,0:T(8,128)S(1)} %shard_map.102.after), channel_id=1, source_target_pairs={{0,2},{2,0},{1,3},{3,1},{4,6},{6,4},{5,7},{7,5},{8,10},{10,8},{9,1... | collective-permute-start | bytes 393224 | tf_op jit(solution)/shard_map/ppermute | solution.py:264
  8.9 4.6 %collective-permute-start.1 = (f32[128,512]{1,0:T(8,128)S(1)}, f32[128,512]{1,0:T(8,128)S(1)}, u32[]{:S(2)}, u32[]{:S(2)}) collective-permute-start(f32[128,512]{1,0:T(8,128)S(1)} %get-tuple-element.47), channel_id=1, source_target_pairs={{0,1},{1,0},{2,3},{3,2},{4,5},{5,4},{6,7},{7,6},{8,9},{9,8},{10,11... | collective-permute-start | bytes 786440 | tf_op jit(solution)/shard_map/ppermute | solution.py:301
  9.0 9.2 %collective-permute-start.2 = (f32[168,128]{1,0:T(8,128)S(1)}, f32[168,128]{1,0:T(8,128)S(1)}, u32[]{:S(2)}, u32[]{:S(2)}) collective-permute-start(f32[168,128]{1,0:T(8,128)S(1)} %get-tuple-element.51), channel_id=1, source_target_pairs={{0,8},{4,12},{8,0},{12,4},{1,9},{5,13},{9,1},{13,5},{2,10},{6,14},... | collective-permute-start | bytes 258056 | tf_op jit(solution)/shard_map/ppermute | solution.py:300
  11.9 9.1 %collective-permute-start.3 = (f32[168,128]{1,0:T(8,128)S(1)}, f32[168,128]{1,0:T(8,128)S(1)}, u32[]{:S(2)}, u32[]{:S(2)}) collective-permute-start(f32[168,128]{1,0:T(8,128)S(1)} %get-tuple-element.52), channel_id=1, source_target_pairs={{0,4},{4,0},{8,12},{12,8},{1,5},{5,1},{9,13},{13,9},{2,6},{6,2},{1... | collective-permute-start | bytes 258056 | tf_op jit(solution)/shard_map/ppermute | solution.py:300
  13.4 7.5 %collective-permute-start.4 = (f32[168,128]{1,0:T(8,128)S(1)}, f32[168,128]{1,0:T(8,128)S(1)}, u32[]{:S(2)}, u32[]{:S(2)}) collective-permute-start(f32[168,128]{1,0:T(8,128)S(1)} %get-tuple-element.53), channel_id=1, source_target_pairs={{0,12},{4,8},{8,4},{12,0},{1,13},{5,9},{9,5},{13,1},{2,14},{6,10},... | collective-permute-start | bytes 258056 | tf_op jit(solution)/shard_map/ppermute | solution.py:300
  13.7 15.8 %collective-permute-start.6 = (f32[112,256]{1,0:T(8,128)S(1)}, f32[112,256]{1,0:T(8,128)S(1)}, u32[]{:S(2)}, u32[]{:S(2)}) collective-permute-start(f32[112,256]{1,0:T(8,128)S(1)} %get-tuple-element.57), channel_id=1, source_target_pairs={{0,4},{4,0},{8,12},{12,8},{1,5},{5,1},{9,13},{13,9},{2,6},{6,2},{1... | collective-permute-start | bytes 344072 | tf_op jit(solution)/shard_map/ppermute | solution.py:310
  14.7 14.8 %collective-permute-start.7 = (f32[112,256]{1,0:T(8,128)S(1)}, f32[112,256]{1,0:T(8,128)S(1)}, u32[]{:S(2)}, u32[]{:S(2)}) collective-permute-start(f32[112,256]{1,0:T(8,128)S(1)} %get-tuple-element.58), channel_id=1, source_target_pairs={{0,8},{4,12},{8,0},{12,4},{1,9},{5,13},{9,1},{13,5},{2,10},{6,14},... | collective-permute-start | bytes 344072 | tf_op jit(solution)/shard_map/ppermute | solution.py:310
  18.2 11.3 %collective-permute-start.8 = (f32[112,256]{1,0:T(8,128)S(1)}, f32[112,256]{1,0:T(8,128)S(1)}, u32[]{:S(2)}, u32[]{:S(2)}) collective-permute-start(f32[112,256]{1,0:T(8,128)S(1)} %get-tuple-element.59), channel_id=1, source_target_pairs={{0,12},{4,8},{8,4},{12,0},{1,13},{5,9},{9,5},{13,1},{2,14},{6,10},... | collective-permute-start | bytes 344072 | tf_op jit(solution)/shard_map/ppermute | solution.py:310
  21.0 1.6 %collective-permute-start.9 = (f32[80,256]{1,0:T(8,128)S(1)}, f32[80,256]{1,0:T(8,128)S(1)}, u32[]{:S(2)}, u32[]{:S(2)}) collective-permute-start(f32[80,256]{1,0:T(8,128)S(1)} %get-tuple-element.60.own), channel_id=1, source_target_pairs={{0,1},{1,0},{2,3},{3,2},{4,5},{5,4},{6,7},{7,6},{8,9},{9,8},{10,11... | collective-permute-start | bytes 245768 | tf_op jit(solution)/shard_map/ppermute | solution.py:318
  21.1 8.4 %collective-permute-start.5 = (f32[136,128]{1,0:T(8,128)S(1)}, f32[136,128]{1,0:T(8,128)S(1)}, u32[]{:S(2)}, u32[]{:S(2)}) collective-permute-start(f32[136,128]{1,0:T(8,128)S(1)} %get-tuple-element.56), channel_id=1, source_target_pairs={{0,2},{2,0},{1,3},{3,1},{4,6},{6,4},{5,7},{7,5},{8,10},{10,8},{9,1... | collective-permute-start | bytes 208904 | tf_op jit(solution)/shard_map/ppermute | solution.py:319
  29.6 1.5 %collective-permute-start.10 = (f32[80,256]{1,0:T(8,128)S(1)}, f32[80,256]{1,0:T(8,128)S(1)}, u32[]{:S(2)}, u32[]{:S(2)}) collective-permute-start(f32[80,256]{1,0:T(8,128)S(1)} %get-tuple-element.63.own), channel_id=1, source_target_pairs={{0,1},{1,0},{2,3},{3,2},{4,5},{5,4},{6,7},{7,6},{8,9},{9,8},{10,11... | collective-permute-start | bytes 245768 | tf_op jit(solution)/shard_map/ppermute | solution.py:336

commit v5 on v4

--- a/solution.py
+++ b/solution.py
@@ -350,7 +350,7 @@
         (second, second_other, table, row_mine, plane, col, core),
         "vvvvvvh",
         "hhhh",
-        scratch=[pltpu.VMEM((8, 8, rest, bb), F32), dma((8,)), pltpu.VMEM((rb, ni), F32), dma((3,))],
+        scratch=[pltpu.VMEM((16, 4, rest, bb), F32), dma((16,)), pltpu.VMEM((rb, ni), F32), dma((3,))],
         cost=(3 * nc * rest * bb, 4 * nc * rest * bb),
         input_output_aliases={6: 0},
     )

time: 35.9 us -> 35.9 us (level)
  no operation moved by 1% of the time
where the time goes in v5:
time: 35.9 us; the launch traced here: 35.8 us
  Pallas kernels  17.4 us (48%)
  starting transfers between devices  16.6 us (46%)
  waiting for transfers between devices  1.02 us (3%)
  between operations  0.75 us (2%)
    pallas_call x9, Pallas kernels, call(): pl.pallas_call(kernel, out_shape=[s if hasattr(s, 'dtype') else jax.Shape...  17.4 us
    ppermute x6, starting transfers between devices, direct(): lax.ppermute(s, 'bx', pairs(nbx, i))  11.7 us
    ppermute x2, starting transfers between devices, direct(): x_in = lax.ppermute(x_send, 'by', pairs(nby, 1))  4.55 us
    ppermute x2, waiting for transfers between devices, direct(): x_in = lax.ppermute(x_send, 'by', pairs(nby, 1))  1 us
  transfers between devices with their start and end apart: 11, of which 1 were waited for; matrix products, arithmetic and copies ran while one was open for 0% of the time, Pallas kernels for 30%

profile of v5, /device:TPU:0, one launch (start us, length us, event | category | flops | bytes accessed | tf_op | source)
XLA Modules:
  0.0 35.8 jit_solution(11176620231602832280)
XLA Ops:
  0.6 1.5 %shard_map.102.after = f32[256,128]{1,0:T(8,128)S(1)} custom-call(f32[1,128,512]{2,1,0:T(8,128)} %slab.3, f32[512,512]{1,0:T(8,128)} %cols.3), custom_call_target="tpu_custom_call" | custom-call | flops 100663296 | bytes 786432 | tf_op jit(solution)/shard_map/pallas_call | solution.py:45
  2.1 3.0 %collective-permute-start = (f32[256,128]{1,0:T(8,128)S(1)}, f32[256,128]{1,0:T(8,128)S(1)}, u32[]{:S(2)}, u32[]{:S(2)}) collective-permute-start(f32[256,128]{1,0:T(8,128)S(1)} %shard_map.102.after), channel_id=1, source_target_pairs={{0,2},{2,0},{1,3},{3,1},{4,6},{6,4},{5,7},{7,5},{8,10},{10,8},{9,1... | collective-permute-start | bytes 393224 | tf_op jit(solution)/shard_map/ppermute | solution.py:264
  5.1 2.5 %shard_map.103 = (f32[256,128]{1,0:T(8,128)S(1)}, f32[128,128]{1,0:T(8,128)S(1)}, f32[128,128]{1,0:T(8,128)S(1)}, f32[8,128]{1,0:T(8,128)S(1)}, f32[128,512]{1,0...) custom-call(f32[1,128,512]{2,1,0:T(8,128)} %slab.3, ...), custom_call_target="tpu_custom_call" | custom-call | flops 301989888 | bytes 1310720 | tf_op jit(solution)/shard_map/pallas_call | solution.py:45
  7.6 1.0 %collective-permute-done.received = f32[256,128]{1,0:T(8,128)S(1)} collective-permute-done((f32[256,128]{1,0:T(8,128)S(1)}, f32[256,128]{1,0:T(8,128)S(1)}, u32[]{:S(2)}, u32[]{:S(2)}) %collective-permute-start) | collective-permute-done | bytes 131104 | tf_op jit(solution)/shard_map/ppermute | solution.py:264
  8.6 0.3 shard_map.104
  8.9 0.1 collective-permute-start.1
  9.0 2.9 %collective-permute-start.2 = (f32[168,128]{1,0:T(8,128)S(1)}, f32[168,128]{1,0:T(8,128)S(1)}, u32[]{:S(2)}, u32[]{:S(2)}) collective-permute-start(f32[168,128]{1,0:T(8,128)S(1)} %get-tuple-element.51), channel_id=1, source_target_pairs={{0,8},{4,12},{8,0},{12,4},{1,9},{5,13},{9,1},{13,5},{2,10},{6,14},... | collective-permute-start | bytes 258056 | tf_op jit(solution)/shard_map/ppermute | solution.py:300
  11.9 1.6 %collective-permute-start.3 = (f32[168,128]{1,0:T(8,128)S(1)}, f32[168,128]{1,0:T(8,128)S(1)}, u32[]{:S(2)}, u32[]{:S(2)}) collective-permute-start(f32[168,128]{1,0:T(8,128)S(1)} %get-tuple-element.52), channel_id=1, source_target_pairs={{0,4},{4,0},{8,12},{12,8},{1,5},{5,1},{9,13},{13,9},{2,6},{6,2},{1... | collective-permute-start | bytes 258056 | tf_op jit(solution)/shard_map/ppermute | solution.py:300
  13.4 0.0 collective-permute-start.4
  13.4 0.0 collective-permute-done.1.col_received
  13.4 0.3 shard_map.105
  13.7 1.0 %collective-permute-start.6 = (f32[112,256]{1,0:T(8,128)S(1)}, f32[112,256]{1,0:T(8,128)S(1)}, u32[]{:S(2)}, u32[]{:S(2)}) collective-permute-start(f32[112,256]{1,0:T(8,128)S(1)} %get-tuple-element.57), channel_id=1, source_target_pairs={{0,4},{4,0},{8,12},{12,8},{1,5},{5,1},{9,13},{13,9},{2,6},{6,2},{1... | collective-permute-start | bytes 344072 | tf_op jit(solution)/shard_map/ppermute | solution.py:310
  14.7 3.5 %collective-permute-start.7 = (f32[112,256]{1,0:T(8,128)S(1)}, f32[112,256]{1,0:T(8,128)S(1)}, u32[]{:S(2)}, u32[]{:S(2)}) collective-permute-start(f32[112,256]{1,0:T(8,128)S(1)} %get-tuple-element.58), channel_id=1, source_target_pairs={{0,8},{4,12},{8,0},{12,4},{1,9},{5,13},{9,1},{13,5},{2,10},{6,14},... | collective-permute-start | bytes 344072 | tf_op jit(solution)/shard_map/ppermute | solution.py:310
  18.2 0.0 collective-permute-done.2.in_a
  18.2 2.8 %collective-permute-start.8 = (f32[112,256]{1,0:T(8,128)S(1)}, f32[112,256]{1,0:T(8,128)S(1)}, u32[]{:S(2)}, u32[]{:S(2)}) collective-permute-start(f32[112,256]{1,0:T(8,128)S(1)} %get-tuple-element.59), channel_id=1, source_target_pairs={{0,12},{4,8},{8,4},{12,0},{1,13},{5,9},{9,5},{13,1},{2,14},{6,10},... | collective-permute-start | bytes 344072 | tf_op jit(solution)/shard_map/ppermute | solution.py:310
  21.0 0.0 collective-permute-done.3.in_b
  21.0 0.0 collective-permute-done.4.in_c
  21.0 0.1 collective-permute-start.9
  21.1 1.6 %collective-permute-start.5 = (f32[136,128]{1,0:T(8,128)S(1)}, f32[136,128]{1,0:T(8,128)S(1)}, u32[]{:S(2)}, u32[]{:S(2)}) collective-permute-start(f32[136,128]{1,0:T(8,128)S(1)} %get-tuple-element.56), channel_id=1, source_target_pairs={{0,2},{2,0},{1,3},{3,1},{4,6},{6,4},{5,7},{7,5},{8,10},{10,8},{9,1... | collective-permute-start | bytes 208904 | tf_op jit(solution)/shard_map/ppermute | solution.py:319
  22.6 0.0 collective-permute-done.9.other
  22.6 6.8 %shard_map.107 = (f32[256,128,256]{2,1,0:T(8,128)}, f32[8,128]{1,0:T(8,128)S(1)}) custom-call(f32[80,256]{1,0:T(8,128)S(1)} %get-tuple-element.60.own, f32[80,256]{1,0:T(8,128)S(1)} %collective-permute-done.9.other, f32[2,256,256]{2,1,0:T(8,128)S(1)} %get-tuple-element.61.table), custom_call_target="tpu_custom_call" | custom-call | flops 14745600 | bytes 19660800 | tf_op jit(solution)/shard_map/pallas_call | solution.py:45
  29.5 0.0 collective-permute-done.5.x_received
  29.5 0.0 collective-permute-done.6.in_a
  29.5 0.0 collective-permute-done.7.in_b
  29.5 0.0 collective-permute-done.8.in_c
  29.6 0.2 collective-permute-start.10
  29.8 1.2 %shard_map.109.core = f32[256,128,256]{2,1,0:T(8,128)} custom-call(f32[80,256]{1,0:T(8,128)S(1)} %get-tuple-element.60.own, f32[80,256]{1,0:T(8,128)S(1)} %collective-permute-done.9.other, f32[2,256,256]{2,1,0:T(8,128)S(1)} %get-tuple-element.61.table, f32[256,128,256]{2,1,0:T(8,128)} %get-tuple-element.67.core), custom_call_target="tpu_custom_call", output_to_operand_aliasing={{}: (3, {})} | custom-call | flops 983040 | bytes 1310720 | tf_op jit(solution)/shard_map/pallas_call | solution.py:45
  31.0 0.0 collective-permute-done.10.other
  31.0 4.7 %shard_map.110 = (f32[256,128,256]{2,1,0:T(8,128)}, f32[1,256]{1,0:T(1,128)}, f32[64,128]{1,0:T(8,128)}, f32[32,512]{1,0:T(8,128)}) custom-call(f32[80,256]{1,0:T(8,128)S(1)} %get-tuple-element.63.own, f32[80,256]{1,0:T(8,128)S(1)} %collective-permute-done.10.other, f32[2,256,256]{2,1,0:T(8,128)S(1)} %get-tuple-element.61.table, ...), custom_call_target="tpu_custom_call", output_to_operand_aliasing={{0}: (6, {})} | custom-call | flops 9437184 | bytes 12582912 | tf_op jit(solution)/shard_map/pallas_call | solution.py:45
  (2 shorter events, 0.1 us)
Async XLA Ops:
  2.1 6.5 %collective-permute-start = (f32[256,128]{1,0:T(8,128)S(1)}, f32[256,128]{1,0:T(8,128)S(1)}, u32[]{:S(2)}, u32[]{:S(2)}) collective-permute-start(f32[256,128]{1,0:T(8,128)S(1)} %shard_map.102.after), channel_id=1, source_target_pairs={{0,2},{2,0},{1,3},{3,1},{4,6},{6,4},{5,7},{7,5},{8,10},{10,8},{9,1... | collective-permute-start | bytes 393224 | tf_op jit(solution)/shard_map/ppermute | solution.py:264
  8.9 4.6 %collective-permute-start.1 = (f32[128,512]{1,0:T(8,128)S(1)}, f32[128,512]{1,0:T(8,128)S(1)}, u32[]{:S(2)}, u32[]{:S(2)}) collective-permute-start(f32[128,512]{1,0:T(8,128)S(1)} %get-tuple-element.47), channel_id=1, source_target_pairs={{0,1},{1,0},{2,3},{3,2},{4,5},{5,4},{6,7},{7,6},{8,9},{9,8},{10,11... | collective-permute-start | bytes 786440 | tf_op jit(solution)/shard_map/ppermute | solution.py:301
  9.0 9.2 %collective-permute-start.2 = (f32[168,128]{1,0:T(8,128)S(1)}, f32[168,128]{1,0:T(8,128)S(1)}, u32[]{:S(2)}, u32[]{:S(2)}) collective-permute-start(f32[168,128]{1,0:T(8,128)S(1)} %get-tuple-element.51), channel_id=1, source_target_pairs={{0,8},{4,12},{8,0},{12,4},{1,9},{5,13},{9,1},{13,5},{2,10},{6,14},... | collective-permute-start | bytes 258056 | tf_op jit(solution)/shard_map/ppermute | solution.py:300
  11.9 9.1 %collective-permute-start.3 = (f32[168,128]{1,0:T(8,128)S(1)}, f32[168,128]{1,0:T(8,128)S(1)}, u32[]{:S(2)}, u32[]{:S(2)}) collective-permute-start(f32[168,128]{1,0:T(8,128)S(1)} %get-tuple-element.52), channel_id=1, source_target_pairs={{0,4},{4,0},{8,12},{12,8},{1,5},{5,1},{9,13},{13,9},{2,6},{6,2},{1... | collective-permute-start | bytes 258056 | tf_op jit(solution)/shard_map/ppermute | solution.py:300
  13.4 7.5 %collective-permute-start.4 = (f32[168,128]{1,0:T(8,128)S(1)}, f32[168,128]{1,0:T(8,128)S(1)}, u32[]{:S(2)}, u32[]{:S(2)}) collective-permute-start(f32[168,128]{1,0:T(8,128)S(1)} %get-tuple-element.53), channel_id=1, source_target_pairs={{0,12},{4,8},{8,4},{12,0},{1,13},{5,9},{9,5},{13,1},{2,14},{6,10},... | collective-permute-start | bytes 258056 | tf_op jit(solution)/shard_map/ppermute | solution.py:300
  13.7 15.8 %collective-permute-start.6 = (f32[112,256]{1,0:T(8,128)S(1)}, f32[112,256]{1,0:T(8,128)S(1)}, u32[]{:S(2)}, u32[]{:S(2)}) collective-permute-start(f32[112,256]{1,0:T(8,128)S(1)} %get-tuple-element.57), channel_id=1, source_target_pairs={{0,4},{4,0},{8,12},{12,8},{1,5},{5,1},{9,13},{13,9},{2,6},{6,2},{1... | collective-permute-start | bytes 344072 | tf_op jit(solution)/shard_map/ppermute | solution.py:310
  14.7 14.8 %collective-permute-start.7 = (f32[112,256]{1,0:T(8,128)S(1)}, f32[112,256]{1,0:T(8,128)S(1)}, u32[]{:S(2)}, u32[]{:S(2)}) collective-permute-start(f32[112,256]{1,0:T(8,128)S(1)} %get-tuple-element.58), channel_id=1, source_target_pairs={{0,8},{4,12},{8,0},{12,4},{1,9},{5,13},{9,1},{13,5},{2,10},{6,14},... | collective-permute-start | bytes 344072 | tf_op jit(solution)/shard_map/ppermute | solution.py:310
  18.2 11.3 %collective-permute-start.8 = (f32[112,256]{1,0:T(8,128)S(1)}, f32[112,256]{1,0:T(8,128)S(1)}, u32[]{:S(2)}, u32[]{:S(2)}) collective-permute-start(f32[112,256]{1,0:T(8,128)S(1)} %get-tuple-element.59), channel_id=1, source_target_pairs={{0,12},{4,8},{8,4},{12,0},{1,13},{5,9},{9,5},{13,1},{2,14},{6,10},... | collective-permute-start | bytes 344072 | tf_op jit(solution)/shard_map/ppermute | solution.py:310
  21.0 1.6 %collective-permute-start.9 = (f32[80,256]{1,0:T(8,128)S(1)}, f32[80,256]{1,0:T(8,128)S(1)}, u32[]{:S(2)}, u32[]{:S(2)}) collective-permute-start(f32[80,256]{1,0:T(8,128)S(1)} %get-tuple-element.60.own), channel_id=1, source_target_pairs={{0,1},{1,0},{2,3},{3,2},{4,5},{5,4},{6,7},{7,6},{8,9},{9,8},{10,11... | collective-permute-start | bytes 245768 | tf_op jit(solution)/shard_map/ppermute | solution.py:318
  21.1 8.4 %collective-permute-start.5 = (f32[136,128]{1,0:T(8,128)S(1)}, f32[136,128]{1,0:T(8,128)S(1)}, u32[]{:S(2)}, u32[]{:S(2)}) collective-permute-start(f32[136,128]{1,0:T(8,128)S(1)} %get-tuple-element.56), channel_id=1, source_target_pairs={{0,2},{2,0},{1,3},{3,1},{4,6},{6,4},{5,7},{7,5},{8,10},{10,8},{9,1... | collective-permute-start | bytes 208904 | tf_op jit(solution)/shard_map/ppermute | solution.py:319
  29.6 1.5 %collective-permute-start.10 = (f32[80,256]{1,0:T(8,128)S(1)}, f32[80,256]{1,0:T(8,128)S(1)}, u32[]{:S(2)}, u32[]{:S(2)}) collective-permute-start(f32[80,256]{1,0:T(8,128)S(1)} %get-tuple-element.63.own), channel_id=1, source_target_pairs={{0,1},{1,0},{2,3},{3,2},{4,5},{5,4},{6,7},{7,6},{8,9},{9,8},{10,11... | collective-permute-start | bytes 245768 | tf_op jit(solution)/shard_map/ppermute | solution.py:336
